TPU v7x, 256 devices: a whole 4x4x8 slice. The times are simulated.
256 devices in a mesh: store: 16 (over x, y), head: 16 (over z, core).
Axes of the slice: x: 4, y: 4, z: 8, core: 2. Of those that a mesh axis runs over, the one named last changes fastest.
Arguments:
- queries: bfloat16 [64, 1024, 4096], P('store', None, 'head'), may hold values from -64 to 64
- kv_store: bfloat16 [128, 2, 64, 4096], P('store', None, None, 'head'), may hold values from -6 to 6
- hidden_rows: bfloat16 [64, 128, 8192], P('store', None, 'head'), may hold values from -6 to 6
- w_kv: bfloat16 [8192, 2, 4096], P('store', None, 'head'), may hold values from -0.0625 to 0.0625
- passage_ids: int32 [64, 16], replicated, may hold values from 0 to 127, as said below
- passage_home: int32 [128], replicated, may hold values from 0 to 127, as said below
- passage_counts: int32 [64], replicated, may hold values from 8 to 16, as said below
- recompute_pos: int32 [64, 128], P('store'), may hold values from 0 to 1023, as said below
Outputs:
- attended: bfloat16 [64, 1024, 4096], P('store', None, 'head')
Inputs may be any that keep to these rules, and one draw needn't show every extreme that they name: passage_home: a permutation; passage p lies in row passage_home[p] of kv_store, on store device passage_home[p] // 8. passage_ids: the 16 passages of one request are distinct, and every store device holds exactly 1 of them; slots at or past passage_counts are named but not used. passage_counts: some request uses all 16 slots. recompute_pos: the 128 positions of one request are distinct and lie below passage_counts times 64.
All inputs are finite; a program needn't handle non-finite values.
Results may differ from a plain program's by a relative error of at most 0.0054.
Values may be sent and summed in bfloat16 or wider, within the bound.
A program may use at most 128 MiB of HBM per device.

v0:
```python
import jax
import jax.numpy as jnp
from jax import lax
from jax.sharding import PartitionSpec as P

HD = 128


EPS = 1e-06


def normalize(hidden):
    widened = hidden.astype(jnp.float32)
    inv_rms = lax.rsqrt(jnp.mean(widened * widened, axis=-1, keepdims=True) + EPS)
    return (widened * inv_rms).astype(jnp.bfloat16)


def attend(query_rows, context, positions, recomputed, used_slots):
    slot_count, _, block_len, feat_width = context.shape
    key_rows = context[:, 0].reshape(slot_count * block_len, feat_width)
    value_rows = context[:, 1].reshape(slot_count * block_len, feat_width)
    key_rows = key_rows.at[positions].set(recomputed[:, :feat_width])
    value_rows = value_rows.at[positions].set(recomputed[:, feat_width:])
    head_count = feat_width // HD
    query_heads = query_rows.reshape(query_rows.shape[0], head_count, HD)
    key_heads = key_rows.reshape(-1, head_count, HD)
    value_heads = value_rows.reshape(-1, head_count, HD)
    scores = jnp.einsum(
        "qhd,khd->hqk", query_heads, key_heads, preferred_element_type=jnp.float32
    ) * HD ** (-0.5)
    usable = jnp.arange(slot_count * block_len) < used_slots * block_len
    scores = jnp.where(usable[None, None, :], scores, -jnp.inf)
    largest = jnp.max(scores, axis=-1, keepdims=True)
    exps = jnp.exp(scores - largest)
    attn_weights = (exps / jnp.sum(exps, axis=-1, keepdims=True)).astype(jnp.bfloat16)
    mixed = jnp.einsum(
        "hqk,khd->qhd", attn_weights, value_heads, preferred_element_type=jnp.float32
    )
    return mixed.reshape(query_rows.shape[0], feat_width).astype(jnp.bfloat16)


def local(
    queries, kv_store, hidden_rows, w_kv, passage_ids, passage_home, passage_counts, recompute_pos
):
    my_index = lax.axis_index("store")
    local_reqs, sel_rows, _ = hidden_rows.shape
    feat_width = kv_store.shape[-1]
    whole_rows = lax.all_gather(hidden_rows, "head", axis=2, tiled=True)
    normed = normalize(whole_rows.reshape(local_reqs * sel_rows, whole_rows.shape[2]))
    w_piece = lax.all_gather(w_kv, "store", axis=0, tiled=True)
    flat_piece = w_piece.reshape(w_piece.shape[0], 2 * feat_width)
    recomputed = jnp.dot(normed, flat_piece, preferred_element_type=jnp.float32)
    recomputed = recomputed.astype(jnp.bfloat16).reshape(local_reqs, sel_rows, 2 * feat_width)
    stored_rows = passage_home[passage_ids]
    my_rows = lax.dynamic_slice_in_dim(stored_rows, my_index * local_reqs, local_reqs, 0)
    everything = lax.all_gather(kv_store, "store", axis=0, tiled=True)
    contexts = everything[my_rows]
    my_counts = lax.dynamic_slice_in_dim(passage_counts, my_index * local_reqs, local_reqs, 0)

    def one_request(inputs):
        query_rows, context, positions, new_rows, used_slots = inputs
        return attend(query_rows, context, positions, new_rows, used_slots)

    return lax.map(one_request, (queries, contexts, recompute_pos, recomputed, my_counts))


def solution(mesh):
    placed = (
        P("store", None, "head"),
        P("store", None, None, "head"),
        P("store", None, "head"),
        P("store", None, "head"),
        P(),
        P(),
        P(),
        P("store", None),
    )
    return jax.shard_map(
        local, mesh=mesh, in_specs=placed, out_specs=P("store", None, "head"), check_vma=False
    )
```

profile of v0, /device:TPU:1, one launch (start us, length us, event | category | flops | bytes accessed | tf_op | source)
XLA Modules:
  0.0 313.2 jit_solution(10247801932519426042)
XLA Ops:
  9.7 6.6 %gather_fusion = s32[1024]{0:T(1024)S(1)} fusion(s32[128]{0:T(128)S(1)} %copy-done, s32[1024]{0:T(1024)S(1)} %broadcast_clamp_fusion), kind=kCustom, calls=%fused_computation | custom fusion | bytes 12288 | tf_op jit(solution)/shard_map/gather | solution.py:54
  16.5 72.9 %all-gather.8.cloned.1.call-done = bf16[8192,2,256]{2,1,0:T(2,128)(2,1)} async-done(((bf16[512,2,256]{2,1,0:T(2,128)(2,1)}), bf16[8192,2,256]{2,1,0:T(2,128)(2,1)}) %all-gather.8.cloned.1.call-update) | async-done | bytes 8388624 | tf_op jit(solution)/shard_map/all_gather | solution.py:50
  89.4 8.0 %copy.38 = bf16[1024,8,2,256]{3,1,2,0:T(8,128)(2,1)} copy(bf16[1024,8,2,256]{3,2,1,0:T(2,128)(2,1)} %bitcast.68) | data formatting | bytes 16777216
  97.4 50.0 %all-gather.6.cloned.1.call-done = bf16[4,128,8192]{2,1,0:T(8,128)(2,1)} async-done(((bf16[4,128,512]{2,1,0:T(8,128)(2,1)}), bf16[4,128,8192]{2,1,0:T(8,128)(2,1)}) %all-gather.6.cloned.1.call-update) | async-done | bytes 8388624 | tf_op jit(solution)/shard_map/all_gather | solution.py:48
  147.3 5.1 %fusion.17 = f32[4,128]{1,0:T(4,128)S(1)} fusion(bf16[4,128,8192]{2,1,0:T(8,128)(2,1)} %all-gather.6.cloned.1.call-done), kind=kLoop, calls=%fused_computation.33 | loop fusion | flops 12582400 | bytes 8390656 | tf_op jit(solution)/shard_map/reduce_sum | solution.py:14
  152.4 9.7 %fusion.18 = bf16[4,128,8192]{2,1,0:T(8,128)(2,1)} fusion(bf16[4,128,8192]{2,1,0:T(8,128)(2,1)} %all-gather.6.cloned.1.call-done, f32[4,128]{1,0:T(4,128)S(1)} %add_rsqrt_fusion), kind=kLoop, calls=%fused_computation.34 | loop fusion | flops 12582912 | bytes 16779264 | tf_op jit(solution)/shard_map/convert_element_type | solution.py:15
  162.2 10.3 %convolution_convert_fusion = bf16[512,512]{1,0:T(8,128)(2,1)S(1)} fusion(bf16[512,8192]{1,0:T(8,128)(2,1)} %bitcast.70, bf16[8192,512]{1,0:T(8,128)(2,1)} %bitcast.69), kind=kOutput, calls=%fused_computation.35 | convolution fusion | flops 4295229440 | bytes 17301504 | tf_op jit(solution)/shard_map/dot_general | solution.py:52
  172.5 51.2 %all-gather.4.cloned.1.call-done = bf16[128,2,64,256]{3,2,1,0:T(8,128)(2,1)} async-done(((bf16[8,2,64,256]{3,2,1,0:T(8,128)(2,1)}), bf16[128,2,64,256]{3,2,1,0:T(8,128)(2,1)}) %all-gather.4.cloned.1.call-update) | async-done | bytes 8388624 | tf_op jit(solution)/shard_map/all_gather | solution.py:56
  223.7 6.2 %gather_fusion.1 = bf16[64,2,64,256]{3,2,1,0:T(8,128)(2,1)} fusion(bf16[128,2,64,256]{3,2,1,0:T(8,128)(2,1)} %all-gather.4.cloned.1.call-done, s32[1024]{0:T(1024)S(1)} %pad_clamp_fusion), kind=kCustom, calls=%fused_computation.1 | custom fusion | bytes 8388864 | tf_op jit(solution)/shard_map/gather | solution.py:57
  229.9 76.8 %while.10 = (s32[]{:T(128)}, bf16[4,1024,256]{2,1,0:T(8,128)(2,1)}, bf16[4,16,2,64,256]{4,3,2,1,0:T(8,128)(2,1)}, s32[4,128]{1,0:T(4,128)}, bf16[4,128,512]{2,1,...) while((s32[]{:T(128)}, bf16[4,1024,256]{2,1,0:T(8,128)(2,1)}, ...), condition=%wide.region_6.7_spmd, body=%wide.region_1.6_spmd.sunk | while | flops 1086589312 | bytes 30822532 | solution.py:64
  229.9 1.3 copy_bitcast_fusion.2
  232.0 1.3 scatter_custom_fusion.11
  236.1 6.2 %fusion.44 = (f32[2,1024]{1,0:T(2,128)S(1)}, f32[2,1024,1024]{1,2,0:T(8,128)}) fusion(pred[1024]{0:T(1024)(128)(4,1)S(1)} %iota_compare_fusion.2, bf16[1024,2,128]{0,2,1:T(8,128)(2,1)S(1)} %bitcast.65, bf16[1024,2,128]{0,2,1:T(8,128)(2,1)S(1)} %bitcast.64), kind=kOutput, calls=%fused_computation.42.clone.1 | convolution fusion | flops 545260544 | bytes 9446400 | tf_op jit(solution)/shard_map/while/body/eval_jaxpr/sub | solution.py:34
  242.3 1.3 scatter_custom_fusion.10
  243.9 4.2 %fusion.45 = bf16[2,128,1024]{2,1,0:T(8,128)(2,1)S(1)} fusion(bf16[1024,2,128]{0,2,1:T(8,128)(2,1)S(1)} %bitcast.66, f32[2,1024,1024]{1,2,0:T(8,128)} %get-tuple-element.131, f32[2,1024]{1,0:T(2,128)S(1)} %get-tuple-element.132), kind=kOutput, calls=%fused_computation.13.clone.1 | convolution fusion | flops 541327360 | bytes 9445376 | tf_op jit(solution)/shard_map/while/body/eval_jaxpr/hqk,khd->qhd/dot_general | solution.py:36
  249.1 1.3 copy_bitcast_fusion.2
  251.2 1.3 scatter_custom_fusion.11
  255.3 6.2 %fusion.44 = (f32[2,1024]{1,0:T(2,128)S(1)}, f32[2,1024,1024]{1,2,0:T(8,128)}) fusion(pred[1024]{0:T(1024)(128)(4,1)S(1)} %iota_compare_fusion.2, bf16[1024,2,128]{0,2,1:T(8,128)(2,1)S(1)} %bitcast.65, bf16[1024,2,128]{0,2,1:T(8,128)(2,1)S(1)} %bitcast.64), kind=kOutput, calls=%fused_computation.42.clone.1 | convolution fusion | flops 545260544 | bytes 9446400 | tf_op jit(solution)/shard_map/while/body/eval_jaxpr/sub | solution.py:34
  261.5 1.3 scatter_custom_fusion.10
  263.1 4.2 %fusion.45 = bf16[2,128,1024]{2,1,0:T(8,128)(2,1)S(1)} fusion(bf16[1024,2,128]{0,2,1:T(8,128)(2,1)S(1)} %bitcast.66, f32[2,1024,1024]{1,2,0:T(8,128)} %get-tuple-element.131, f32[2,1024]{1,0:T(2,128)S(1)} %get-tuple-element.132), kind=kOutput, calls=%fused_computation.13.clone.1 | convolution fusion | flops 541327360 | bytes 9445376 | tf_op jit(solution)/shard_map/while/body/eval_jaxpr/hqk,khd->qhd/dot_general | solution.py:36
  268.3 1.3 copy_bitcast_fusion.2
  270.4 1.3 scatter_custom_fusion.11
  273.2 1.1 constant_dynamic-slice_fusion.7
  274.5 6.2 %fusion.44 = (f32[2,1024]{1,0:T(2,128)S(1)}, f32[2,1024,1024]{1,2,0:T(8,128)}) fusion(pred[1024]{0:T(1024)(128)(4,1)S(1)} %iota_compare_fusion.2, bf16[1024,2,128]{0,2,1:T(8,128)(2,1)S(1)} %bitcast.65, bf16[1024,2,128]{0,2,1:T(8,128)(2,1)S(1)} %bitcast.64), kind=kOutput, calls=%fused_computation.42.clone.1 | convolution fusion | flops 545260544 | bytes 9446400 | tf_op jit(solution)/shard_map/while/body/eval_jaxpr/sub | solution.py:34
  280.7 1.3 scatter_custom_fusion.10
  282.3 4.2 %fusion.45 = bf16[2,128,1024]{2,1,0:T(8,128)(2,1)S(1)} fusion(bf16[1024,2,128]{0,2,1:T(8,128)(2,1)S(1)} %bitcast.66, f32[2,1024,1024]{1,2,0:T(8,128)} %get-tuple-element.131, f32[2,1024]{1,0:T(2,128)S(1)} %get-tuple-element.132), kind=kOutput, calls=%fused_computation.13.clone.1 | convolution fusion | flops 541327360 | bytes 9445376 | tf_op jit(solution)/shard_map/while/body/eval_jaxpr/hqk,khd->qhd/dot_general | solution.py:36
  287.5 1.3 copy_bitcast_fusion.2
  289.6 1.3 scatter_custom_fusion.11
  292.5 1.1 constant_dynamic-slice_fusion.7
  293.8 6.2 %fusion.44 = (f32[2,1024]{1,0:T(2,128)S(1)}, f32[2,1024,1024]{1,2,0:T(8,128)}) fusion(pred[1024]{0:T(1024)(128)(4,1)S(1)} %iota_compare_fusion.2, bf16[1024,2,128]{0,2,1:T(8,128)(2,1)S(1)} %bitcast.65, bf16[1024,2,128]{0,2,1:T(8,128)(2,1)S(1)} %bitcast.64), kind=kOutput, calls=%fused_computation.42.clone.1 | convolution fusion | flops 545260544 | bytes 9446400 | tf_op jit(solution)/shard_map/while/body/eval_jaxpr/sub | solution.py:34
  299.9 1.3 scatter_custom_fusion.10
  301.5 4.2 %fusion.45 = bf16[2,128,1024]{2,1,0:T(8,128)(2,1)S(1)} fusion(bf16[1024,2,128]{0,2,1:T(8,128)(2,1)S(1)} %bitcast.66, f32[2,1024,1024]{1,2,0:T(8,128)} %get-tuple-element.131, f32[2,1024]{1,0:T(2,128)S(1)} %get-tuple-element.132), kind=kOutput, calls=%fused_computation.13.clone.1 | convolution fusion | flops 541327360 | bytes 9445376 | tf_op jit(solution)/shard_map/while/body/eval_jaxpr/hqk,khd->qhd/dot_general | solution.py:36
  (63 shorter events, 17.8 us)
Async XLA Ops:
  6.5 3.1 copy-start
  6.5 82.8 %all-gather.8.cloned.1.call-start = ((), (), s32[]{:S(2)}) async-start(), calls=%async_computation.2 | async-start | bytes 8912896 | tf_op jit(solution)/shard_map/all_gather | solution.py:50
  7.3 140.1 %all-gather.6.cloned.1.call-start = ((), (), s32[]{:S(2)}) async-start(), calls=%async_computation.1 | async-start | bytes 8912896 | tf_op jit(solution)/shard_map/all_gather | solution.py:48
  8.0 215.7 %all-gather.4.cloned.1.call-start = ((), (), s32[]{:S(2)}) async-start(), calls=%async_computation | async-start | bytes 8912896 | tf_op jit(solution)/shard_map/all_gather | solution.py:56
  9.6 6.8 %copy-start.1 = (s32[64]{0:T(128)S(1)}, s32[64]{0:T(128)}, u32[]{:S(2)}) copy-start(s32[64]{0:T(128)} %param.16) | copy-start | bytes 772
Sparse Core Ops, SparseCore 0:
  9.8 79.5 all-gather.7
  91.2 56.0 all-gather.5
  149.8 73.8 all-gather.3
where the time goes:
time: 314 us; the launch traced here: 313 us
  waiting for transfers between devices  176 us (56%)
  matrix products  51.7 us (16%)
  local copies, waits for them, and re-layouts  50.9 us (16%)
  other arithmetic  18.4 us (6%)
  between operations  13.2 us (4%)
    all_gather x1, waiting for transfers between devices, local(): w_piece = lax.all_gather(w_kv, 'store', axis=0, tiled=True)  72.9 us
    all_gather x1, waiting for transfers between devices, local(): everything = lax.all_gather(kv_store, 'store', axis=0, tiled=True)  51.2 us
    all_gather x1, waiting for transfers between devices, local(): whole_rows = lax.all_gather(hidden_rows, 'head', axis=2, tiled=True)  50 us
    sub x4, matrix products, attend(): exps = jnp.exp(scores - largest)  24.7 us
    dot_general x4, matrix products, attend(): jnp.einsum('hqk,khd->qhd', attn_weights, value_heads, preferred_element_t...  16.6 us
    dot_general x1, matrix products, local(): recomputed = jnp.dot(normed, flat_piece, preferred_element_type=jnp.float32)  10.3 us
    convert_element_type x1, other arithmetic, normalize(): return (widened * inv_rms).astype(jnp.bfloat16)  9.72 us
    unnamed x5, local copies, waits for them, and re-layouts  8.01 us
  transfers between devices with their start and end apart: 3, of which 3 were waited for; matrix products, arithmetic and copies ran while one was open for 13% of the time, Pallas kernels for 0%

commit v1 on v0

v1 whole, which is shorter than its diff:
```python
import math

import jax
import jax.numpy as jnp
from jax import lax
from jax.experimental import pallas as pl
from jax.experimental.pallas import tpu as pltpu
from jax.sharding import PartitionSpec as P

MESH = pl.DeviceIdType.MESH

D = 8192
HD = 128
EPS = 1e-06
SLOTS = 16
BLK = 64
SPAN = SLOTS * BLK
REQS = 4
QLEN = 1024
SEL = 128
FEAT = 256
ROWS = REQS * SEL
DEEP = 512
QTILE = 256
MASKED = -1e30
TO_BASE_TWO = HD ** (-0.5) * math.log2(math.e)

NT = (((1,), (1,)), ((), ()))
NN = (((1,), (0,)), ((), ()))


def dot(a, b, dims):
    return lax.dot_general(a, b, dims, preferred_element_type=jnp.float32)


def remote(src, dst, send_sem, recv_sem, device):
    return pltpu.make_async_remote_copy(
        src_ref=src,
        dst_ref=dst,
        send_sem=send_sem,
        recv_sem=recv_sem,
        device_id=device,
        device_id_type=MESH,
    )


class Ring4:
    def __init__(self, at, me, plus, minus, send, recv):
        self.at, self.plus, self.minus, self.send, self.recv = at, plus, minus, send, recv
        self.me, self.prev, self.next, self.far = me, (me + 3) % 4, (me + 1) % 4, (me + 2) % 4

    def copy(self, source, part, k, device):
        piece = self.at(source, part)
        return remote(piece, piece, self.send(k), self.recv(k), device)

    def start(self):
        self.copy(self.me, None, 0, self.plus).start()
        self.copy(self.me, None, 1, self.minus).start()

    def forward(self):
        self.copy(self.prev, None, 0, self.plus).wait_recv()
        self.copy(self.prev, 0, 2, self.plus).start()
        self.copy(self.next, None, 1, self.minus).wait_recv()
        self.copy(self.next, 1, 3, self.minus).start()

    def finish(self):
        self.copy(self.far, 0, 2, self.plus).wait_recv()
        self.copy(self.far, 1, 3, self.minus).wait_recv()

    def drain(self):
        self.copy(self.me, None, 0, self.plus).wait_send()
        self.copy(self.me, None, 1, self.minus).wait_send()
        self.copy(self.prev, 0, 2, self.plus).wait_send()
        self.copy(self.next, 1, 3, self.minus).wait_send()


def kernel(
    q_hbm, kv_hbm, x_hbm, w_hbm, table, bias, out_hbm,
    q, x_all, w_all, k_near, v_near, k_send, v_send, k_all, v_all,
    mixed, top, total, projected, squares, fresh, result,
    local_sem, out_sem, kv1_send, kv1_recv, kv2_send, kv2_recv,
    w1_send, w1_recv, w2_send, w2_recv, x_send, x_recv, pair_send, pair_recv,
):
    store, head = lax.axis_index("store"), lax.axis_index("head")
    x, y, z, core = store // 4, store % 4, head // 2, head % 2

    def at_xy(dx, dy):
        return {"store": ((x + dx) % 4) * 4 + (y + dy) % 4, "head": head}

    def at_z(dz):
        return {"store": store, "head": ((z + dz) % 8) * 2 + core}

    sibling = {"store": store, "head": z * 2 + (1 - core)}

    loads = [
        pltpu.make_async_copy(kv_hbm.at[:, 0], k_near.at[x], local_sem.at[0]),
        pltpu.make_async_copy(kv_hbm.at[:, 1], v_near.at[y], local_sem.at[1]),
        pltpu.make_async_copy(x_hbm, x_all.at[head], local_sem.at[2]),
        pltpu.make_async_copy(w_hbm, w_all.at[store], local_sem.at[3]),
        pltpu.make_async_copy(q_hbm, q, local_sem.at[4]),
    ]
    for load in loads:
        load.start()

    barrier = pltpu.get_barrier_semaphore()
    peers = [at_xy(d, 0) for d in (1, 3, 2)] + [at_xy(0, d) for d in (1, 3, 2)]
    peers += [at_z(1), at_z(7), sibling]
    for peer in peers:
        pl.semaphore_signal(barrier, inc=1, device_id=peer, device_id_type=MESH)
    pl.semaphore_wait(barrier, len(peers))

    def sems(ref, *lead):
        return lambda k: ref.at[(*lead, k)]

    def near_at(buf):
        return lambda i, part: buf.at[i] if part is None else buf.at[i, pl.ds(4 * part, 4)]

    def w_at(block, half):
        def at(i, part):
            first = half * 256 + (0 if part is None else 128 * part)
            return w_all.at[block(i), pl.ds(first, 256 if part is None else 128)]

        return at

    along_x = (x, at_xy(1, 0), at_xy(3, 0))
    along_y = (y, at_xy(0, 1), at_xy(0, 3))
    k1 = Ring4(near_at(k_near), *along_x, sems(kv1_send, 0), sems(kv1_recv, 0))
    v1 = Ring4(near_at(v_near), *along_y, sems(kv1_send, 1), sems(kv1_recv, 1))
    wa1 = Ring4(w_at(lambda i: i * 4 + y, 0), *along_x, sems(w1_send, 0), sems(w1_recv, 0))
    wb1 = Ring4(w_at(lambda i: x * 4 + i, 1), *along_y, sems(w1_send, 1), sems(w1_recv, 1))

    def offset(j):
        return j + j // 2 - 2 * (j // 3)

    def wa2(j):
        xs = (x + offset(j)) % 4
        return Ring4(w_at(lambda i: xs * 4 + i, 0), *along_y, sems(w2_send, 0, j), sems(w2_recv, 0, j))

    def wb2(j):
        ys = (y + offset(j)) % 4
        return Ring4(w_at(lambda i: i * 4 + ys, 1), *along_x, sems(w2_send, 1, j), sems(w2_recv, 1, j))

    def x_block(dz, part=None):
        block = ((z + dz) % 8) * 2 + core
        return x_all.at[block] if part is None else x_all.at[block, pl.ds(256 * part, 256)]

    def x_copy(way, k):
        dz = (8 - k) % 8 if way == 0 else k
        piece = x_block(dz, way if k == 3 else None)
        return remote(piece, piece, x_send.at[way, k], x_recv.at[way, k], at_z(1 if way == 0 else 7))

    def x_arrived(way, k):
        dz = (8 - k) % 8 if way == 0 else k
        piece = x_block(dz, way if k == 4 else None)
        remote(piece, piece, x_send.at[way, k - 1], x_recv.at[way, k - 1], at_z(1)).wait_recv()

    def pair_copy(way, k, other=False):
        dz = (8 - k) % 8 if way == 0 else k
        block = ((z + dz) % 8) * 2 + (1 - core if other else core)
        piece = x_all.at[block, pl.ds(256 * way, 256)] if k == 4 else x_all.at[block]
        return remote(piece, piece, pair_send.at[way, k], pair_recv.at[way, k], sibling)

    def x_step(k):
        for way in (0, 1):
            x_arrived(way, k)
            if k < 4:
                x_copy(way, k).start()
            pair_copy(way, k).start()

    def k2(r, d):
        return remote(
            k_send.at[(y + d) % 4, r], k_all.at[r, y],
            kv2_send.at[0, r, d - 1], kv2_recv.at[0, r, d - 1], at_xy(0, d),
        )

    def k2_arrived(r, d):
        remote(
            k_send.at[0, r], k_all.at[r, (y + 4 - d) % 4],
            kv2_send.at[0, r, d - 1], kv2_recv.at[0, r, d - 1], at_xy(0, d),
        ).wait_recv()

    def v2(r, d):
        return remote(
            v_send.at[(x + d) % 4, r], v_all.at[r, :, x],
            kv2_send.at[1, r, d - 1], kv2_recv.at[1, r, d - 1], at_xy(d, 0),
        )

    def v2_arrived(r, d):
        remote(
            v_send.at[0, r], v_all.at[r, :, (x + 4 - d) % 4],
            kv2_send.at[1, r, d - 1], kv2_recv.at[1, r, d - 1], at_xy(d, 0),
        ).wait_recv()

    loads[0].wait()
    loads[1].wait()
    k1.start()
    v1.start()
    loads[2].wait()
    x_copy(0, 0).start()
    x_copy(1, 0).start()
    pair_copy(0, 0).start()
    loads[3].wait()
    loads[4].wait()
    k1.forward()
    v1.forward()
    wa1.start()
    wb1.start()

    k1.finish()

    @pl.loop(0, REQS)
    def _(r):
        for yd in range(4):
            for xs in range(4):
                row = table[(x * 4 + yd) * REQS + r, xs * 4 + y]
                k_send[yd, r, xs] = k_near[xs, row]
        k_all[r, y] = k_send[y, r]
        for d in (1, 3, 2):
            k2(r, d).start()

    v1.finish()

    @pl.loop(0, REQS)
    def _(r):
        for xd in range(4):
            for ys in range(4):
                row = table[(xd * 4 + y) * REQS + r, x * 4 + ys]
                v_send[xd, r, ys] = v_near[ys, row]
        for ys in range(4):
            v_all[r, ys, x] = v_send[x, r, ys]
        for d in (1, 3, 2):
            v2(r, d).start()

    x_step(1)
    wa1.forward()
    wb1.forward()
    for j in (0, 1, 2):
        wa2(j).start()
        wb2(j).start()
    x_step(2)
    wa1.finish()
    wb1.finish()
    wa2(3).start()
    wb2(3).start()
    x_step(3)
    x_step(4)

    for way, k in ((0, 0), (0, 1), (1, 1), (0, 2), (1, 2), (0, 3), (1, 3), (0, 4), (1, 4)):
        pair_copy(way, k, other=True).wait_recv()

    squares[...] = jnp.zeros_like(squares)
    projected[...] = jnp.zeros_like(projected)

    @pl.loop(0, 16)
    def _(b):
        wide = x_all[b].astype(jnp.float32)
        wide = wide * wide
        squares[...] += (wide[:, 0:128] + wide[:, 128:256]) + (wide[:, 256:384] + wide[:, 384:512])

    def multiply(block, half):
        first = pl.multiple_of(half * 256, 256)
        projected[...] += dot(
            x_all[block, :, pl.ds(first, 256)], w_all[block, pl.ds(first, 256), :], NN
        )

    @pl.loop(0, REQS)
    def _(r):
        for d in (1, 3, 2):
            k2_arrived(r, d)
            v2_arrived(r, d)

        @pl.loop(0, QLEN // QTILE)
        def _(t):
            first = pl.multiple_of(t * QTILE, QTILE)
            shift = bias[r]
            for h in (0, 1):
                lanes = pl.ds(h * HD, HD)
                keys = k_all[r, :, :, :, lanes].reshape(SPAN, HD)
                values = v_all[r, :, :, :, lanes].reshape(SPAN, HD)
                scores = dot(q[r, pl.ds(first, QTILE), lanes], keys, NT) * TO_BASE_TWO + shift
                largest = jnp.max(scores, axis=-1, keepdims=True)
                exps = jnp.exp2(scores - largest)
                summed = jnp.sum(exps, axis=-1, keepdims=True)
                mixed[r, pl.ds(first, QTILE), lanes] = dot(exps.astype(jnp.bfloat16), values, NN)
                top[r, pl.ds(first, QTILE), lanes] = jnp.broadcast_to(largest, (QTILE, HD))
                total[r, pl.ds(first, QTILE), lanes] = jnp.broadcast_to(summed, (QTILE, HD))

        wa2(r).forward()
        wb2(r).forward()
        xs, ys = (x + offset(r)) % 4, (y + offset(r)) % 4

        @pl.loop(0, 3)
        def _(i):
            multiply(xs * 4 + (y + 3 + i) % 4, 0)
            multiply(((x + 3 + i) % 4) * 4 + ys, 1)

    @pl.loop(0, 4)
    def _(j):
        xs, ys = (x + offset(j)) % 4, (y + offset(j)) % 4
        wa2(j).finish()
        multiply(xs * 4 + (y + 2) % 4, 0)
        wb2(j).finish()
        multiply(((x + 2) % 4) * 4 + ys, 1)

    mean = jnp.sum(squares[...], axis=-1, keepdims=True) * (1.0 / D)
    fresh[...] = (projected[...] * lax.rsqrt(mean + EPS)).astype(jnp.bfloat16)

    @pl.loop(0, REQS)
    def _(r):
        rows = pl.ds(pl.multiple_of(r * SEL, SEL), SEL)
        for h in (0, 1):
            lanes = pl.ds(h * HD, HD)
            scores = dot(q[r, :, lanes], fresh[rows, lanes], NT) * TO_BASE_TWO
            before = top[r, :, lanes]
            largest = jnp.maximum(before, jnp.max(scores, axis=-1, keepdims=True))
            exps = jnp.exp2(scores - largest)
            fade = jnp.exp2(before - largest)
            summed = total[r, :, lanes] * fade + jnp.sum(exps, axis=-1, keepdims=True)
            gained = dot(exps.astype(jnp.bfloat16), fresh[rows, pl.ds(FEAT + h * HD, HD)], NN)
            attended = (mixed[r, :, lanes] * fade + gained) / summed
            result[r, :, lanes] = attended.astype(jnp.bfloat16)
        pltpu.make_async_copy(result.at[r], out_hbm.at[r], out_sem.at[r]).start()

    for ring in (k1, v1, wa1, wb1):
        ring.drain()

    @pl.loop(0, 4)
    def _(j):
        wa2(j).drain()
        wb2(j).drain()
        for d in (1, 2, 3):
            k2(j, d).wait_send()
            v2(j, d).wait_send()

    for way in (0, 1):
        for k in range(4):
            x_copy(way, k).wait_send()
    for way, k in ((0, 0), (0, 1), (1, 1), (0, 2), (1, 2), (0, 3), (1, 3), (0, 4), (1, 4)):
        pair_copy(way, k).wait_send()
    for r in range(REQS):
        pltpu.make_async_copy(result.at[r], out_hbm.at[r], out_sem.at[r]).wait()


def attend(q, kv, rows, weights, table, bias):
    any_ref = pl.BlockSpec(memory_space=pl.ANY)
    bf, f32 = jnp.bfloat16, jnp.float32
    dma = pltpu.SemaphoreType.DMA
    return pl.pallas_call(
        kernel,
        out_shape=jax.ShapeDtypeStruct((REQS, QLEN, FEAT), bf),
        in_specs=[any_ref] * 4
        + [pl.BlockSpec(memory_space=pltpu.SMEM), pl.BlockSpec(memory_space=pltpu.VMEM)],
        out_specs=any_ref,
        scratch_shapes=[
            pltpu.VMEM((REQS, QLEN, FEAT), bf),
            pltpu.VMEM((16, ROWS, DEEP), bf),
            pltpu.VMEM((16, DEEP, 2 * FEAT), bf),
            pltpu.VMEM((4, 8, BLK, FEAT), bf),
            pltpu.VMEM((4, 8, BLK, FEAT), bf),
            pltpu.VMEM((4, REQS, 4, BLK, FEAT), bf),
            pltpu.VMEM((4, REQS, 4, BLK, FEAT), bf),
            pltpu.VMEM((REQS, 4, 4, BLK, FEAT), bf),
            pltpu.VMEM((REQS, 4, 4, BLK, FEAT), bf),
            pltpu.VMEM((REQS, QLEN, FEAT), f32),
            pltpu.VMEM((REQS, QLEN, FEAT), f32),
            pltpu.VMEM((REQS, QLEN, FEAT), f32),
            pltpu.VMEM((ROWS, 2 * FEAT), f32),
            pltpu.VMEM((ROWS, HD), f32),
            pltpu.VMEM((ROWS, 2 * FEAT), bf),
            pltpu.VMEM((REQS, QLEN, FEAT), bf),
            dma((5,)),
            dma((REQS,)),
            dma((2, 4)), dma((2, 4)),
            dma((2, REQS, 3)), dma((2, REQS, 3)),
            dma((2, 4)), dma((2, 4)),
            dma((2, 4, 4)), dma((2, 4, 4)),
            dma((2, 4)), dma((2, 4)),
            dma((2, 5)), dma((2, 5)),
        ],
        compiler_params=pltpu.CompilerParams(
            collective_id=0, has_side_effects=True, vmem_limit_bytes=60 * 1024 * 1024
        ),
        cost_estimate=pl.CostEstimate(
            flops=14_000_000_000, bytes_accessed=8_000_000, transcendentals=10_000_000
        ),
        name="blend",
    )(q, kv, rows, weights, table, bias)


def local(
    queries, kv_store, hidden_rows, w_kv, passage_ids, passage_home, passage_counts, recompute_pos
):
    store = lax.axis_index("store")
    requests = passage_ids.shape[0]
    named = passage_ids[:, :, None] == jnp.arange(passage_home.shape[0])
    stored = jnp.sum(jnp.where(named, passage_home, 0), axis=-1)
    filled = (stored // 8)[:, :, None] == jnp.arange(16)
    slots = jnp.arange(SLOTS)[None, :, None]
    packed = jnp.sum(jnp.where(filled, slots * 8 + (stored % 8)[:, :, None], 0), axis=1)
    table = packed % 8
    mine = lax.dynamic_slice_in_dim(packed, store * REQS, REQS, 0) // 8
    counts = lax.dynamic_slice_in_dim(passage_counts, store * REQS, REQS, 0)
    mine = mine.reshape(REQS, 4, 4).transpose(0, 2, 1).reshape(REQS, SLOTS)
    place = (mine[:, :, None] * BLK + jnp.arange(BLK)).reshape(REQS, SPAN)
    renewed = jnp.any(place[:, None, :] == recompute_pos[:, :, None], axis=1)
    dropped = renewed | (place >= counts[:, None] * BLK)
    bias = jnp.where(dropped, MASKED, 0.0).astype(jnp.float32).reshape(REQS, 1, SPAN)
    return attend(
        queries,
        kv_store,
        hidden_rows.reshape(ROWS, DEEP),
        w_kv.reshape(DEEP, 2 * FEAT),
        table,
        bias,
    )


def solution(mesh):
    placed = (
        P("store", None, "head"),
        P("store", None, None, "head"),
        P("store", None, "head"),
        P("store", None, "head"),
        P(),
        P(),
        P(),
        P("store", None),
    )
    return jax.shard_map(
        local, mesh=mesh, in_specs=placed, out_specs=P("store", None, "head"), check_vma=False
    )
```

time: 314 us -> 110 us (0.35)
  waiting for transfers between devices: 176 us -> 0 us
  Pallas kernels: 0 us -> 97.7 us
  matrix products: 51.7 us -> 0 us
  local copies, waits for them, and re-layouts: 50.9 us -> 6.56 us
  other arithmetic: 18.4 us -> 5.21 us
  between operations: 13.2 us -> 0.05 us
    all_gather x3 -> x0, waiting for transfers between devices: 174 us -> none  [the longest x1 72.9 us: local(): w_piece = lax.all_gather(w_kv, 'store', axis=0, tiled=True)]
    pallas_call x0 -> x1, Pallas kernels: none -> 97.7 us  [attend(): pl.pallas_call(kernel, out_shape=jax.ShapeDtypeStruct((REQS, QLEN, FEAT),...]
    dot_general x5 -> x0, matrix products: 27 us -> none  [the longest x4 16.6 us: attend(): jnp.einsum('hqk,khd->qhd', attn_weights, value_heads, preferred_element_t...]
    sub x4 -> x0, matrix products: 24.7 us -> none  [attend(): exps = jnp.exp(scores - largest)]
    gather x3 -> x0, local copies, waits for them, and re-layouts: 12.8 us -> none  [the longest x2 6.64 us: local(): stored_rows = passage_home[passage_ids]]
    scatter x12 -> x0, local copies, waits for them, and re-layouts: 11.6 us -> none  [the longest x8 6.21 us: attend(): key_rows = key_rows.at[positions].set(recomputed[:, :feat_width])]
    convert_element_type x1 -> x0, other arithmetic: 9.72 us -> none  [normalize(): return (widened * inv_rms).astype(jnp.bfloat16)]
    dynamic_slice x13 -> x0, local copies, waits for them, and re-layouts: 7.69 us -> none  [the longest x12 7.61 us: local(): lax.map(one_request, (queries, contexts, recompute_pos, recomputed, my_co...]
  transfers between devices with their start and end apart: 3 -> 0, of which waited for: 3 -> 0; matrix products, arithmetic and copies ran while one was open for 13% -> 0% of each run, Pallas kernels for 0% -> 0%
where the time goes in v1:
time: 110 us
  Pallas kernels  97.7 us (89%)
  local copies, waits for them, and re-layouts  6.56 us (6%)
  other arithmetic  5.21 us (5%)
    pallas_call x1, Pallas kernels, attend(): pl.pallas_call(kernel, out_shape=jax.ShapeDtypeStruct((REQS, QLEN, FEAT),...  97.7 us
    unnamed x3, local copies, waits for them, and re-layouts  5.74 us

profile of v1, /device:TPU:1, one launch (start us, length us, event | category | flops | bytes accessed | tf_op | source)
XLA Modules:
  0.0 109.5 jit_solution(13341267559310685102)
XLA Ops:
  0.0 0.7 dynamic-slice_multiply_fusion
  0.7 0.1 add.85
  0.8 0.8 copy.23
  1.6 2.0 %select_reduce_fusion = s32[64,16]{1,0:T(8,128)S(1)} fusion(s32[128]{0:T(128)} %param.13, s32[64,16]{1,0:T(8,128)S(1)} %copy.23), kind=kLoop, calls=%fused_computation.1 | loop fusion | flops 392192 | bytes 8704 | tf_op jit(solution)/shard_map/reduce_sum | solution.py:396
  3.6 0.1 copy.24
  3.7 0.1 copy.26
  3.8 0.1 copy.27
  3.9 0.6 add_select_fusion.table
  4.5 0.1 mul.40
  4.6 0.1 copy.31
  4.7 0.1 mul.42
  4.8 0.1 add.82
  4.8 0.1 add.88
  4.9 0.1 add.83
  5.0 1.1 %compare_reduce_fusion = pred[4,1024]{1,0:T(4,128)(4,1)S(1)} fusion(s32[4,128]{1,0:T(4,128)} %param.15, s32[4,1024]{1,0:T(4,128)S(1)} %broadcast_add_fusion), kind=kLoop, calls=%fused_computation | loop fusion | flops 1044480 | bytes 22528 | tf_op jit(solution)/shard_map/reduce_or | solution.py:405
  6.2 0.7 fusion.bias
  6.8 1.9 %copy.33 = bf16[64,8,2,256]{3,1,2,0:T(8,128)(2,1)} copy(bf16[64,8,2,256]{3,2,1,0:T(2,128)(2,1)} %bitcast.5) | data formatting | bytes 1048576
  8.8 97.7 %blend.1 = bf16[4,1024,256]{2,1,0:T(8,128)(2,1)} custom-call(bf16[4,1024,256]{2,1,0:T(8,128)(2,1)} %q_hbm.1, bf16[8,2,64,256]{3,2,1,0:T(8,128)(2,1)} %kv_hbm.1, bf16[512,512]{1,0:T(8,128)(2,1)} %bitcast.9, bf16[512,512]{1,0:T(8,128)(2,1)} %bitcast.6, s32[64,16]{1,0:T(8,128)} %add_select_fusion.table, f32[4,1,1024]{2,1,0:T(1,128)} %fusion.bias), custom_call_target="tpu_custom_call" | custom-call | flops 14000000000 | bytes 8000000 | tf_op jit(solution)/shard_map/blend/pallas_call | solution.py:348
  106.5 3.0 %copy.38 = bf16[4,1024,256]{2,1,0:T(8,128)(2,1)} copy(bf16[4,1024,256]{2,1,0:T(8,128)(2,1)} %blend.1) | data formatting | bytes 4194304
  (6 shorter events, 0.1 us)

commit v2 on v1

--- a/solution.py
+++ b/solution.py
@@ -75,8 +75,8 @@
 
 
 def kernel(
-    q_hbm, kv_hbm, x_hbm, w_hbm, table, bias, out_hbm,
-    q, x_all, w_all, k_near, v_near, k_send, v_send, k_all, v_all,
+    q_hbm, kv_hbm, x_hbm, w_hbm, ids_hbm, home_hbm, counts_hbm, renewed_hbm, out_hbm,
+    ids, home, counts, renewed, q, w_raw, packed, table, bias, x_all, w_all, k_near, v_near, k_send, v_send, k_all, v_all,
     mixed, top, total, projected, squares, fresh, result,
     local_sem, out_sem, kv1_send, kv1_recv, kv2_send, kv2_recv,
     w1_send, w1_recv, w2_send, w2_recv, x_send, x_recv, pair_send, pair_recv,
@@ -96,8 +96,12 @@
         pltpu.make_async_copy(kv_hbm.at[:, 0], k_near.at[x], local_sem.at[0]),
         pltpu.make_async_copy(kv_hbm.at[:, 1], v_near.at[y], local_sem.at[1]),
         pltpu.make_async_copy(x_hbm, x_all.at[head], local_sem.at[2]),
-        pltpu.make_async_copy(w_hbm, w_all.at[store], local_sem.at[3]),
+        pltpu.make_async_copy(w_hbm, w_raw, local_sem.at[3]),
         pltpu.make_async_copy(q_hbm, q, local_sem.at[4]),
+        pltpu.make_async_copy(ids_hbm, ids, local_sem.at[5]),
+        pltpu.make_async_copy(home_hbm, home, local_sem.at[6]),
+        pltpu.make_async_copy(counts_hbm, counts, local_sem.at[7]),
+        pltpu.make_async_copy(renewed_hbm, renewed, local_sem.at[8]),
     ]
     for load in loads:
         load.start()
@@ -190,6 +194,37 @@
             v_send.at[0, r], v_all.at[r, :, (x + 4 - d) % 4],
             kv2_send.at[1, r, d - 1], kv2_recv.at[1, r, d - 1], at_xy(d, 0),
         ).wait_recv()
+
+    def name_rows():
+        named = ids[...]
+        stored = lax.fori_loop(
+            0, 128, lambda p, rows: jnp.where(named == p, home[p], rows), named, unroll=8
+        )
+        device = lax.broadcasted_iota(jnp.int32, (SLOTS, 64), 0)
+        filled = jnp.zeros((SLOTS, 64), jnp.int32)
+        for j in range(SLOTS):
+            row = stored[j : j + 1, :]
+            filled = jnp.where(device == (row >> 3), j * 8 + (row & 7), filled)
+        packed[...] = jnp.zeros_like(packed)
+        packed[:, pl.ds(0, 64)] = filled
+        move = pltpu.make_async_copy(packed, table, local_sem.at[9])
+        move.start()
+        move.wait()
+
+    def mask_positions():
+        lane = lax.broadcasted_iota(jnp.int32, (1, SPAN), 1)
+        block, inner = lane >> 6, lane & 63
+        for r in range(REQS):
+            mine = store * REQS + r
+            place = jnp.zeros((1, SPAN), jnp.int32)
+            for b in range(SLOTS):
+                slot = table[(b % 4) * 4 + b // 4, mine] // 8
+                place = jnp.where(block == b, slot * BLK, place)
+            place = place + inner
+            shift = jnp.where(place < counts[mine] * BLK, 0.0, MASKED)
+            bias[r] = lax.fori_loop(
+                0, SEL, lambda i, kept: jnp.where(place == renewed[r, i], MASKED, kept), shift, unroll=8
+            )
 
     loads[0].wait()
     loads[1].wait()
@@ -199,8 +234,12 @@
     x_copy(0, 0).start()
     x_copy(1, 0).start()
     pair_copy(0, 0).start()
+    loads[5].wait()
+    loads[6].wait()
+    name_rows()
     loads[3].wait()
-    loads[4].wait()
+    w_all[store, :, pl.ds(0, FEAT)] = w_raw[:, 0, :]
+    w_all[store, :, pl.ds(FEAT, FEAT)] = w_raw[:, 1, :]
     k1.forward()
     v1.forward()
     wa1.start()
@@ -212,7 +251,7 @@
     def _(r):
         for yd in range(4):
             for xs in range(4):
-                row = table[(x * 4 + yd) * REQS + r, xs * 4 + y]
+                row = table[xs * 4 + y, (x * 4 + yd) * REQS + r] % 8
                 k_send[yd, r, xs] = k_near[xs, row]
         k_all[r, y] = k_send[y, r]
         for d in (1, 3, 2):
@@ -224,7 +263,7 @@
     def _(r):
         for xd in range(4):
             for ys in range(4):
-                row = table[(xd * 4 + y) * REQS + r, x * 4 + ys]
+                row = table[x * 4 + ys, (xd * 4 + y) * REQS + r] % 8
                 v_send[xd, r, ys] = v_near[ys, row]
         for ys in range(4):
             v_all[r, ys, x] = v_send[x, r, ys]
@@ -248,6 +287,10 @@
     for way, k in ((0, 0), (0, 1), (1, 1), (0, 2), (1, 2), (0, 3), (1, 3), (0, 4), (1, 4)):
         pair_copy(way, k, other=True).wait_recv()
 
+    loads[4].wait()
+    loads[7].wait()
+    loads[8].wait()
+    mask_positions()
     squares[...] = jnp.zeros_like(squares)
     projected[...] = jnp.zeros_like(projected)
 
@@ -341,18 +384,25 @@
         pltpu.make_async_copy(result.at[r], out_hbm.at[r], out_sem.at[r]).wait()
 
 
-def attend(q, kv, rows, weights, table, bias):
-    any_ref = pl.BlockSpec(memory_space=pl.ANY)
+def attend(q, kv, rows, weights, ids, home, counts, renewed):
+    hbm = pl.BlockSpec(memory_space=pltpu.HBM)
     bf, f32 = jnp.bfloat16, jnp.float32
     dma = pltpu.SemaphoreType.DMA
     return pl.pallas_call(
         kernel,
         out_shape=jax.ShapeDtypeStruct((REQS, QLEN, FEAT), bf),
-        in_specs=[any_ref] * 4
-        + [pl.BlockSpec(memory_space=pltpu.SMEM), pl.BlockSpec(memory_space=pltpu.VMEM)],
-        out_specs=any_ref,
+        in_specs=[hbm] * 8,
+        out_specs=pl.BlockSpec(memory_space=pl.ANY),
         scratch_shapes=[
+            pltpu.VMEM((SLOTS, 64), jnp.int32),
+            pltpu.SMEM((128,), jnp.int32),
+            pltpu.SMEM((64,), jnp.int32),
+            pltpu.SMEM((REQS, SEL), jnp.int32),
             pltpu.VMEM((REQS, QLEN, FEAT), bf),
+            pltpu.VMEM((DEEP, 2, FEAT), bf),
+            pltpu.VMEM((SLOTS, 128), jnp.int32),
+            pltpu.SMEM((SLOTS, 128), jnp.int32),
+            pltpu.VMEM((REQS, 1, SPAN), f32),
             pltpu.VMEM((16, ROWS, DEEP), bf),
             pltpu.VMEM((16, DEEP, 2 * FEAT), bf),
             pltpu.VMEM((4, 8, BLK, FEAT), bf),
@@ -368,7 +418,7 @@
             pltpu.VMEM((ROWS, HD), f32),
             pltpu.VMEM((ROWS, 2 * FEAT), bf),
             pltpu.VMEM((REQS, QLEN, FEAT), bf),
-            dma((5,)),
+            dma((10,)),
             dma((REQS,)),
             dma((2, 4)), dma((2, 4)),
             dma((2, REQS, 3)), dma((2, REQS, 3)),
@@ -384,34 +434,21 @@
             flops=14_000_000_000, bytes_accessed=8_000_000, transcendentals=10_000_000
         ),
         name="blend",
-    )(q, kv, rows, weights, table, bias)
+    )(q, kv, rows, weights, ids, home, counts, renewed)
 
 
 def local(
     queries, kv_store, hidden_rows, w_kv, passage_ids, passage_home, passage_counts, recompute_pos
 ):
-    store = lax.axis_index("store")
-    requests = passage_ids.shape[0]
-    named = passage_ids[:, :, None] == jnp.arange(passage_home.shape[0])
-    stored = jnp.sum(jnp.where(named, passage_home, 0), axis=-1)
-    filled = (stored // 8)[:, :, None] == jnp.arange(16)
-    slots = jnp.arange(SLOTS)[None, :, None]
-    packed = jnp.sum(jnp.where(filled, slots * 8 + (stored % 8)[:, :, None], 0), axis=1)
-    table = packed % 8
-    mine = lax.dynamic_slice_in_dim(packed, store * REQS, REQS, 0) // 8
-    counts = lax.dynamic_slice_in_dim(passage_counts, store * REQS, REQS, 0)
-    mine = mine.reshape(REQS, 4, 4).transpose(0, 2, 1).reshape(REQS, SLOTS)
-    place = (mine[:, :, None] * BLK + jnp.arange(BLK)).reshape(REQS, SPAN)
-    renewed = jnp.any(place[:, None, :] == recompute_pos[:, :, None], axis=1)
-    dropped = renewed | (place >= counts[:, None] * BLK)
-    bias = jnp.where(dropped, MASKED, 0.0).astype(jnp.float32).reshape(REQS, 1, SPAN)
     return attend(
         queries,
         kv_store,
         hidden_rows.reshape(ROWS, DEEP),
-        w_kv.reshape(DEEP, 2 * FEAT),
-        table,
-        bias,
+        w_kv,
+        passage_ids.T,
+        passage_home,
+        passage_counts,
+        recompute_pos,
     )
 
 

time: 110 us -> 102 us (0.927)
  other arithmetic: 5.21 us -> 0 us
  local copies, waits for them, and re-layouts: 6.56 us -> 3.05 us
    unnamed x3 -> x1, local copies, waits for them, and re-layouts: 5.74 us -> 3.05 us
    reduce_sum x2 -> x0, other arithmetic: 2.01 us -> none  [the longest x1 1.96 us: local(): stored = jnp.sum(jnp.where(named, passage_home, 0), axis=-1)]
    select_n x3 -> x0, other arithmetic: 1.34 us -> none  [the longest x1 0.69 us: local(): jnp.where(dropped, MASKED, 0.0).astype(jnp.float32).reshape(REQS, 1, SPAN)]
    reduce_or x1 -> x0, other arithmetic: 1.11 us -> none  [local(): renewed = jnp.any(place[:, None, :] == recompute_pos[:, :, None], axis=1)]
where the time goes in v2:
time: 102 us
  Pallas kernels  98.6 us (97%)
  local copies, waits for them, and re-layouts  3.05 us (3%)
    pallas_call x1, Pallas kernels, attend(): pl.pallas_call(kernel, out_shape=jax.ShapeDtypeStruct((REQS, QLEN, FEAT),...  98.6 us
    unnamed x1, local copies, waits for them, and re-layouts  3.05 us

profile of v2, /device:TPU:1, one launch (start us, length us, event | category | flops | bytes accessed | tf_op | source)
XLA Modules:
  0.0 101.7 jit_solution(15637290381105165915)
XLA Ops:
  0.0 98.6 %blend.1 = bf16[4,1024,256]{2,1,0:T(8,128)(2,1)} custom-call(bf16[4,1024,256]{2,1,0:T(8,128)(2,1)} %q_hbm.1, bf16[8,2,64,256]{3,2,1,0:T(8,128)(2,1)} %kv_hbm.1, bf16[512,512]{1,0:T(8,128)(2,1)} %bitcast.2, bf16[512,2,256]{2,1,0:T(2,128)(2,1)} %w_hbm.1, s32[16,64]{1,0:T(8,128)} %bitcast.3, s32[128]{0:T(128)} %home_hbm.1, s32[64]{0:T(128)} %counts_hbm.1, ...), custom_call_target="tpu_custom_call" | custom-call | flops 14000000000 | bytes 8000000 | tf_op jit(solution)/shard_map/blend/pallas_call | solution.py:391
  98.6 3.0 %copy.10 = bf16[4,1024,256]{2,1,0:T(8,128)(2,1)} copy(bf16[4,1024,256]{2,1,0:T(8,128)(2,1)} %blend.1) | data formatting | bytes 4194304

commit v3 on v2

--- a/solution.py
+++ b/solution.py
@@ -22,7 +22,7 @@
 ROWS = REQS * SEL
 DEEP = 512
 QTILE = 256
-MASKED = -1e30
+MASKED = -1e28
 TO_BASE_TWO = HD ** (-0.5) * math.log2(math.e)
 
 NT = (((1,), (1,)), ((), ()))
@@ -76,10 +76,12 @@
 
 def kernel(
     q_hbm, kv_hbm, x_hbm, w_hbm, ids_hbm, home_hbm, counts_hbm, renewed_hbm, out_hbm,
-    ids, home, counts, renewed, q, w_raw, packed, table, bias, x_all, w_all, k_near, v_near, k_send, v_send, k_all, v_all,
-    mixed, top, total, projected, squares, fresh, result,
+    ids, home, counts, renewed, q, w_raw, packed, table, bias, x_own, x_all, w_all, k_near, v_near, k_send, v_send, k_all, v_all,
+    mixed, top, total, projected, squares, part_send, part_recv, norm_send, norm_recv, fresh, result,
+    wide_q, wide_k, wide_v,
     local_sem, out_sem, kv1_send, kv1_recv, kv2_send, kv2_recv,
-    w1_send, w1_recv, w2_send, w2_recv, x_send, x_recv, pair_send, pair_recv,
+    own_send, own_recv, other_send, other_recv, side_send, side_recv, flow_send, flow_recv,
+    lend_send, lend_recv, core_send, core_recv, sum_send, sum_recv,
 ):
     store, head = lax.axis_index("store"), lax.axis_index("head")
     x, y, z, core = store // 4, store % 4, head // 2, head % 2
@@ -92,10 +94,17 @@
 
     sibling = {"store": store, "head": z * 2 + (1 - core)}
 
+    half_of, odd = y // 2, y % 2
+    source = z % 2 == half_of
+    relay = z % 2 != half_of
+    ally = {"store": x * 4 + y + 1 - 2 * odd, "head": head}
+    partner = {"store": x * 4 + 3 - y, "head": head}
+    x_mine = (z // 2) * 2 + core
+    w_mine = x * 2 + odd
+
     loads = [
         pltpu.make_async_copy(kv_hbm.at[:, 0], k_near.at[x], local_sem.at[0]),
         pltpu.make_async_copy(kv_hbm.at[:, 1], v_near.at[y], local_sem.at[1]),
-        pltpu.make_async_copy(x_hbm, x_all.at[head], local_sem.at[2]),
         pltpu.make_async_copy(w_hbm, w_raw, local_sem.at[3]),
         pltpu.make_async_copy(q_hbm, q, local_sem.at[4]),
         pltpu.make_async_copy(ids_hbm, ids, local_sem.at[5]),
@@ -105,6 +114,10 @@
     ]
     for load in loads:
         load.start()
+    x_load = pltpu.make_async_copy(x_hbm, x_all.at[x_mine, pl.ds(0, ROWS)], local_sem.at[2])
+    x_lent = pltpu.make_async_copy(x_hbm, x_own, local_sem.at[2])
+    pl.when(source)(x_load.start)
+    pl.when(relay)(x_lent.start)
 
     barrier = pltpu.get_barrier_semaphore()
     peers = [at_xy(d, 0) for d in (1, 3, 2)] + [at_xy(0, d) for d in (1, 3, 2)]
@@ -119,10 +132,11 @@
     def near_at(buf):
         return lambda i, part: buf.at[i] if part is None else buf.at[i, pl.ds(4 * part, 4)]
 
-    def w_at(block, half):
+    def w_at(side, first, rows):
         def at(i, part):
-            first = half * 256 + (0 if part is None else 128 * part)
-            return w_all.at[block(i), pl.ds(first, 256 if part is None else 128)]
+            if part is None:
+                return w_all.at[i * 2 + side, pl.ds(first, rows)]
+            return w_all.at[i * 2 + side, pl.ds(first + part * (rows // 2), rows // 2)]
 
         return at
 
@@ -130,46 +144,154 @@
     along_y = (y, at_xy(0, 1), at_xy(0, 3))
     k1 = Ring4(near_at(k_near), *along_x, sems(kv1_send, 0), sems(kv1_recv, 0))
     v1 = Ring4(near_at(v_near), *along_y, sems(kv1_send, 1), sems(kv1_recv, 1))
-    wa1 = Ring4(w_at(lambda i: i * 4 + y, 0), *along_x, sems(w1_send, 0), sems(w1_recv, 0))
-    wb1 = Ring4(w_at(lambda i: x * 4 + i, 1), *along_y, sems(w1_send, 1), sems(w1_recv, 1))
+    own = Ring4(w_at(odd, 0, DEEP), *along_x, sems(own_send), sems(own_recv))
+    other = Ring4(w_at(1 - odd, 0, DEEP // 2), *along_x, sems(other_send), sems(other_recv))
 
     def offset(j):
         return j + j // 2 - 2 * (j // 3)
 
-    def wa2(j):
-        xs = (x + offset(j)) % 4
-        return Ring4(w_at(lambda i: xs * 4 + i, 0), *along_y, sems(w2_send, 0, j), sems(w2_recv, 0, j))
-
-    def wb2(j):
-        ys = (y + offset(j)) % 4
-        return Ring4(w_at(lambda i: i * 4 + ys, 1), *along_x, sems(w2_send, 1, j), sems(w2_recv, 1, j))
-
-    def x_block(dz, part=None):
-        block = ((z + dz) % 8) * 2 + core
-        return x_all.at[block] if part is None else x_all.at[block, pl.ds(256 * part, 256)]
-
-    def x_copy(way, k):
-        dz = (8 - k) % 8 if way == 0 else k
-        piece = x_block(dz, way if k == 3 else None)
-        return remote(piece, piece, x_send.at[way, k], x_recv.at[way, k], at_z(1 if way == 0 else 7))
-
-    def x_arrived(way, k):
-        dz = (8 - k) % 8 if way == 0 else k
-        piece = x_block(dz, way if k == 4 else None)
-        remote(piece, piece, x_send.at[way, k - 1], x_recv.at[way, k - 1], at_z(1)).wait_recv()
-
-    def pair_copy(way, k, other=False):
-        dz = (8 - k) % 8 if way == 0 else k
-        block = ((z + dz) % 8) * 2 + (1 - core if other else core)
-        piece = x_all.at[block, pl.ds(256 * way, 256)] if k == 4 else x_all.at[block]
-        return remote(piece, piece, pair_send.at[way, k], pair_recv.at[way, k], sibling)
-
-    def x_step(k):
-        for way in (0, 1):
-            x_arrived(way, k)
-            if k < 4:
-                x_copy(way, k).start()
-            pair_copy(way, k).start()
+    def side(j, sent=True):
+        block = (x + offset(j % 4)) % 4 * 2 + (odd if sent else 1 - odd)
+        piece = w_all.at[block, pl.ds(0 if j == 4 else DEEP // 2, DEEP // 2)]
+        return remote(piece, piece, side_send.at[j], side_recv.at[j], ally)
+
+    def x_piece(way, dist, w):
+        at = (z + (8 - dist if way == 0 else dist)) % 8
+        return x_all.at[(at // 2) * 2 + core, pl.ds(256 * w, 256)]
+
+    def flow(way, stage, dist, w):
+        piece = x_piece(way, dist, w)
+        device = at_z(1 if way == 0 else 7)
+        return remote(piece, piece, flow_send.at[way, stage, w], flow_recv.at[way, stage, w], device)
+
+    def lend(half):
+        return remote(
+            x_own.at[pl.ds(256 * half, 256)], x_all.at[x_mine, pl.ds(ROWS + 256 * half, 256)],
+            lend_send.at[half], lend_recv.at[half], partner,
+        )
+
+    def to_core(dist, part, mine=True):
+        at = (z + 8 + dist) % 8
+        piece = x_all.at[(at // 2) * 2 + (core if mine else 1 - core), pl.ds(ROWS * part, ROWS)]
+        return remote(piece, piece, core_send.at[at // 2, part], core_recv.at[at // 2, part], sibling)
+
+    def x_start():
+        @pl.when(source)
+        def _():
+            x_load.wait()
+            for w in (0, 1):
+                flow(0, 0, 0, w).start()
+                flow(1, 0, 0, w).start()
+            to_core(0, 0).start()
+
+        @pl.when(relay)
+        def _():
+            x_lent.wait()
+            lend(0).start()
+            lend(1).start()
+
+    def x_one():
+        @pl.when(relay)
+        def _():
+            for w in (0, 1):
+                for way in (0, 1):
+                    flow(way, 0, 1, w).wait_recv()
+                    flow(way, 0, 1, w).start()
+            to_core(-1, 0).start()
+            to_core(1, 0).start()
+
+        @pl.when(source)
+        def _():
+            for w in (2, 3):
+                lend(w - 2).wait_recv()
+                flow(0, 0, 0, w).start()
+                flow(1, 0, 0, w).start()
+            to_core(0, 1).start()
+
+    def x_two(half):
+        w = 2 + half
+
+        @pl.when(relay)
+        def _():
+            for way in (0, 1):
+                flow(way, 0, 1, w).wait_recv()
+                flow(way, 0, 1, w).start()
+            if half:
+                to_core(-1, 1).start()
+                to_core(1, 1).start()
+
+        @pl.when(source)
+        def _():
+            for way in (0, 1):
+                flow(way, 0, 2, half).wait_recv()
+            if half:
+                to_core(-2, 0).start()
+                to_core(2, 0).start()
+
+    def x_three(half):
+        w = 2 + half
+
+        @pl.when(source)
+        def _():
+            for way in (0, 1):
+                flow(way, 0, 2, w).wait_recv()
+                flow(way, 1, 2, w).start()
+            if half:
+                for way in (0, 1):
+                    flow(way, 1, 2, 0).start()
+                    flow(way, 1, 2, 1).start()
+                to_core(-2, 1).start()
+                to_core(2, 1).start()
+
+    def x_relayed(part):
+        @pl.when(relay)
+        def _():
+            for half in (0, 1):
+                w = 2 * part + half
+                for way in (0, 1):
+                    flow(way, 1, 3, w).wait_recv()
+                    if way == half:
+                        flow(way, 1, 3, w).start()
+            to_core(-3, part).start()
+            to_core(3, part).start()
+
+    def x_ended(part):
+        @pl.when(source)
+        def _():
+            for way in (0, 1):
+                flow(way, 1, 4, 2 * part + way).wait_recv()
+            to_core(4, part).start()
+
+    def x_others(part):
+        for at in range(4):
+            piece = x_all.at[at * 2 + 1 - core, pl.ds(ROWS * part, ROWS)]
+            remote(piece, piece, core_send.at[at, part], core_recv.at[at, part], sibling).wait_recv()
+
+    def x_drain():
+        @pl.when(source)
+        def _():
+            for way in (0, 1):
+                for w in range(4):
+                    flow(way, 0, 0, w).wait_send()
+                    flow(way, 1, 2, w).wait_send()
+
+        @pl.when(relay)
+        def _():
+            lend(0).wait_send()
+            lend(1).wait_send()
+            for way in (0, 1):
+                for w in range(4):
+                    flow(way, 0, 1, w).wait_send()
+                for part in (0, 1):
+                    flow(way, 1, 3, 2 * part + way).wait_send()
+
+        for at in range(4):
+            for part in (0, 1):
+                piece = x_all.at[at * 2 + core, pl.ds(ROWS * part, ROWS)]
+                remote(piece, piece, core_send.at[at, part], core_recv.at[at, part], sibling).wait_send()
+
+    swap = remote(part_send, part_recv, sum_send.at[0], sum_recv.at[0], partner)
+    swap_norm = remote(norm_send, norm_recv, sum_send.at[1], sum_recv.at[1], partner)
 
     def k2(r, d):
         return remote(
@@ -226,88 +348,30 @@
                 0, SEL, lambda i, kept: jnp.where(place == renewed[r, i], MASKED, kept), shift, unroll=8
             )
 
-    loads[0].wait()
-    loads[1].wait()
-    k1.start()
-    v1.start()
-    loads[2].wait()
-    x_copy(0, 0).start()
-    x_copy(1, 0).start()
-    pair_copy(0, 0).start()
-    loads[5].wait()
-    loads[6].wait()
-    name_rows()
-    loads[3].wait()
-    w_all[store, :, pl.ds(0, FEAT)] = w_raw[:, 0, :]
-    w_all[store, :, pl.ds(FEAT, FEAT)] = w_raw[:, 1, :]
-    k1.forward()
-    v1.forward()
-    wa1.start()
-    wb1.start()
-
-    k1.finish()
-
-    @pl.loop(0, REQS)
-    def _(r):
-        for yd in range(4):
-            for xs in range(4):
-                row = table[xs * 4 + y, (x * 4 + yd) * REQS + r] % 8
-                k_send[yd, r, xs] = k_near[xs, row]
-        k_all[r, y] = k_send[y, r]
-        for d in (1, 3, 2):
-            k2(r, d).start()
-
-    v1.finish()
-
-    @pl.loop(0, REQS)
-    def _(r):
-        for xd in range(4):
+    def send_keys(first, count):
+        @pl.loop(first, first + count)
+        def _(r):
+            for yd in range(4):
+                for xs in range(4):
+                    row = table[xs * 4 + y, (x * 4 + yd) * REQS + r] % 8
+                    k_send[yd, r, xs] = k_near[xs, row]
+            k_all[r, y] = k_send[y, r]
+            for d in (1, 3, 2):
+                k2(r, d).start()
+
+    def send_values(first, count):
+        @pl.loop(first, first + count)
+        def _(r):
+            for xd in range(4):
+                for ys in range(4):
+                    row = table[x * 4 + ys, (xd * 4 + y) * REQS + r] % 8
+                    v_send[xd, r, ys] = v_near[ys, row]
             for ys in range(4):
-                row = table[x * 4 + ys, (xd * 4 + y) * REQS + r] % 8
-                v_send[xd, r, ys] = v_near[ys, row]
-        for ys in range(4):
-            v_all[r, ys, x] = v_send[x, r, ys]
-        for d in (1, 3, 2):
-            v2(r, d).start()
-
-    x_step(1)
-    wa1.forward()
-    wb1.forward()
-    for j in (0, 1, 2):
-        wa2(j).start()
-        wb2(j).start()
-    x_step(2)
-    wa1.finish()
-    wb1.finish()
-    wa2(3).start()
-    wb2(3).start()
-    x_step(3)
-    x_step(4)
-
-    for way, k in ((0, 0), (0, 1), (1, 1), (0, 2), (1, 2), (0, 3), (1, 3), (0, 4), (1, 4)):
-        pair_copy(way, k, other=True).wait_recv()
-
-    loads[4].wait()
-    loads[7].wait()
-    loads[8].wait()
-    mask_positions()
-    squares[...] = jnp.zeros_like(squares)
-    projected[...] = jnp.zeros_like(projected)
-
-    @pl.loop(0, 16)
-    def _(b):
-        wide = x_all[b].astype(jnp.float32)
-        wide = wide * wide
-        squares[...] += (wide[:, 0:128] + wide[:, 128:256]) + (wide[:, 256:384] + wide[:, 384:512])
-
-    def multiply(block, half):
-        first = pl.multiple_of(half * 256, 256)
-        projected[...] += dot(
-            x_all[block, :, pl.ds(first, 256)], w_all[block, pl.ds(first, 256), :], NN
-        )
-
-    @pl.loop(0, REQS)
-    def _(r):
+                v_all[r, ys, x] = v_send[x, r, ys]
+            for d in (1, 3, 2):
+                v2(r, d).start()
+
+    def attend_cached(r):
         for d in (1, 3, 2):
             k2_arrived(r, d)
             v2_arrived(r, d)
@@ -328,25 +392,101 @@
                 top[r, pl.ds(first, QTILE), lanes] = jnp.broadcast_to(largest, (QTILE, HD))
                 total[r, pl.ds(first, QTILE), lanes] = jnp.broadcast_to(summed, (QTILE, HD))
 
-        wa2(r).forward()
-        wb2(r).forward()
-        xs, ys = (x + offset(r)) % 4, (y + offset(r)) % 4
-
-        @pl.loop(0, 3)
-        def _(i):
-            multiply(xs * 4 + (y + 3 + i) % 4, 0)
-            multiply(((x + 3 + i) % 4) * 4 + ys, 1)
-
-    @pl.loop(0, 4)
-    def _(j):
-        xs, ys = (x + offset(j)) % 4, (y + offset(j)) % 4
-        wa2(j).finish()
-        multiply(xs * 4 + (y + 2) % 4, 0)
-        wb2(j).finish()
-        multiply(((x + 2) % 4) * 4 + ys, 1)
-
-    mean = jnp.sum(squares[...], axis=-1, keepdims=True) * (1.0 / D)
-    fresh[...] = (projected[...] * lax.rsqrt(mean + EPS)).astype(jnp.bfloat16)
+    def project(part):
+        projected[...] = jnp.zeros_like(projected)
+
+        @pl.loop(0, 8)
+        def _(b):
+            projected[...] += dot(x_all[b, pl.ds(ROWS * part, ROWS), :], w_all[b], NN)
+
+    x_start()
+    loads[0].wait()
+    k1.start()
+    loads[1].wait()
+    v1.start()
+    loads[2].wait()
+    w_all[w_mine, :, pl.ds(0, FEAT)] = w_raw[:, 0, :]
+    w_all[w_mine, :, pl.ds(FEAT, FEAT)] = w_raw[:, 1, :]
+    side(4).start()
+    loads[4].wait()
+    loads[5].wait()
+    name_rows()
+    k1.forward()
+    own.start()
+    side(0).start()
+    k1.finish()
+    send_keys(0, 1)
+    x_one()
+    v1.forward()
+    side(4, False).wait_recv()
+    other.start()
+    x_two(0)
+    own.forward()
+    side(1).start()
+    side(2).start()
+    x_two(1)
+    v1.finish()
+    send_values(0, 1)
+    x_three(0)
+    loads[3].wait()
+    loads[6].wait()
+    loads[7].wait()
+    mask_positions()
+    other.forward()
+    x_three(1)
+    own.finish()
+    side(3).start()
+    send_keys(1, 3)
+    send_values(1, 3)
+    x_relayed(1)
+    attend_cached(0)
+    x_ended(1)
+    other.finish()
+    for j in range(4):
+        side(j, False).wait_recv()
+    x_others(1)
+
+    norm_send[...] = jnp.zeros_like(norm_send)
+
+    @pl.loop(0, 8)
+    def _(b):
+        narrow = x_all[b, pl.ds(ROWS, ROWS), :]
+        norm_send[...] += dot(jnp.ones((8, DEEP), jnp.bfloat16), narrow * narrow, NT)
+
+    project(1)
+    part_send[...] = projected[...].astype(jnp.bfloat16)
+    swap.start()
+    swap_norm.start()
+    x_relayed(0)
+    attend_cached(1)
+    x_ended(0)
+    x_others(0)
+    squares[...] = jnp.zeros_like(squares)
+
+    @pl.loop(0, 8)
+    def _(b):
+        wide = x_all[b, pl.ds(0, ROWS), :].astype(jnp.float32)
+        wide = wide * wide
+        squares[...] += (wide[:, 0:128] + wide[:, 128:256]) + (wide[:, 256:384] + wide[:, 384:512])
+
+    project(0)
+
+    @pl.loop(2, REQS)
+    def _(r):
+        attend_cached(r)
+
+    swap.wait_recv()
+    swap_norm.wait_recv()
+    lent = jnp.transpose(jnp.broadcast_to(norm_recv[0:1, :], (HD, ROWS)))
+    mean = (jnp.sum(squares[...], axis=-1, keepdims=True) + lent) * (1.0 / D)
+    scale = lax.rsqrt(mean + EPS)
+    for i in range(4):
+        lanes = pl.ds(i * HD, HD)
+        summed = projected[:, lanes] + part_recv[:, lanes].astype(jnp.float32)
+        at = i * HD if i < 2 else FEAT + (i - 2) * 2 * HD
+        fresh[:, pl.ds(at, HD)] = (summed * scale).astype(jnp.bfloat16)
+        if i >= 2:
+            fresh[:, pl.ds(at + HD, HD)] = jnp.ones((ROWS, HD), jnp.bfloat16)
 
     @pl.loop(0, REQS)
     def _(r):
@@ -358,28 +498,25 @@
             largest = jnp.maximum(before, jnp.max(scores, axis=-1, keepdims=True))
             exps = jnp.exp2(scores - largest)
             fade = jnp.exp2(before - largest)
-            summed = total[r, :, lanes] * fade + jnp.sum(exps, axis=-1, keepdims=True)
-            gained = dot(exps.astype(jnp.bfloat16), fresh[rows, pl.ds(FEAT + h * HD, HD)], NN)
-            attended = (mixed[r, :, lanes] * fade + gained) / summed
+            both = dot(exps.astype(jnp.bfloat16), fresh[rows, pl.ds(FEAT + h * 2 * HD, 2 * HD)], NN)
+            attended = (mixed[r, :, lanes] * fade + both[:, 0:HD]) / (total[r, :, lanes] * fade + both[:, HD:])
             result[r, :, lanes] = attended.astype(jnp.bfloat16)
         pltpu.make_async_copy(result.at[r], out_hbm.at[r], out_sem.at[r]).start()
 
-    for ring in (k1, v1, wa1, wb1):
+    for ring in (k1, v1, own, other):
         ring.drain()
-
-    @pl.loop(0, 4)
-    def _(j):
-        wa2(j).drain()
-        wb2(j).drain()
+    for j in range(5):
+        side(j).wait_send()
+
+    @pl.loop(0, REQS)
+    def _(r):
         for d in (1, 2, 3):
-            k2(j, d).wait_send()
-            v2(j, d).wait_send()
-
-    for way in (0, 1):
-        for k in range(4):
-            x_copy(way, k).wait_send()
-    for way, k in ((0, 0), (0, 1), (1, 1), (0, 2), (1, 2), (0, 3), (1, 3), (0, 4), (1, 4)):
-        pair_copy(way, k).wait_send()
+            k2(r, d).wait_send()
+            v2(r, d).wait_send()
+
+    x_drain()
+    swap.wait_send()
+    swap_norm.wait_send()
     for r in range(REQS):
         pltpu.make_async_copy(result.at[r], out_hbm.at[r], out_sem.at[r]).wait()
 
@@ -403,8 +540,9 @@
             pltpu.VMEM((SLOTS, 128), jnp.int32),
             pltpu.SMEM((SLOTS, 128), jnp.int32),
             pltpu.VMEM((REQS, 1, SPAN), f32),
-            pltpu.VMEM((16, ROWS, DEEP), bf),
-            pltpu.VMEM((16, DEEP, 2 * FEAT), bf),
+            pltpu.VMEM((ROWS, DEEP), bf),
+            pltpu.VMEM((8, 2 * ROWS, DEEP), bf),
+            pltpu.VMEM((8, DEEP, 2 * FEAT), bf),
             pltpu.VMEM((4, 8, BLK, FEAT), bf),
             pltpu.VMEM((4, 8, BLK, FEAT), bf),
             pltpu.VMEM((4, REQS, 4, BLK, FEAT), bf),
@@ -417,15 +555,25 @@
             pltpu.VMEM((ROWS, 2 * FEAT), f32),
             pltpu.VMEM((ROWS, HD), f32),
             pltpu.VMEM((ROWS, 2 * FEAT), bf),
+            pltpu.VMEM((ROWS, 2 * FEAT), bf),
+            pltpu.VMEM((8, ROWS), f32),
+            pltpu.VMEM((8, ROWS), f32),
+            pltpu.VMEM((ROWS, 3 * FEAT), bf),
             pltpu.VMEM((REQS, QLEN, FEAT), bf),
-            dma((10,)),
+            pltpu.VMEM((2, QLEN, 2 * HD), bf),
+            pltpu.VMEM((2, SPAN, 2 * HD), bf),
+            pltpu.VMEM((2, SPAN, 2 * HD), bf),
+            dma((11,)),
             dma((REQS,)),
             dma((2, 4)), dma((2, 4)),
             dma((2, REQS, 3)), dma((2, REQS, 3)),
-            dma((2, 4)), dma((2, 4)),
-            dma((2, 4, 4)), dma((2, 4, 4)),
-            dma((2, 4)), dma((2, 4)),
-            dma((2, 5)), dma((2, 5)),
+            dma((4,)), dma((4,)),
+            dma((4,)), dma((4,)),
+            dma((5,)), dma((5,)),
+            dma((2, 2, 4)), dma((2, 2, 4)),
+            dma((2,)), dma((2,)),
+            dma((4, 2)), dma((4, 2)),
+            dma((2,)), dma((2,)),
         ],
         compiler_params=pltpu.CompilerParams(
             collective_id=0, has_side_effects=True, vmem_limit_bytes=60 * 1024 * 1024

time: 102 us -> 97.4 us (0.955)
  Pallas kernels: 98.6 us -> 94.3 us
    pallas_call x1, Pallas kernels: 98.6 us -> 94.3 us  [attend(): pl.pallas_call(kernel, out_shape=jax.ShapeDtypeStruct((REQS, QLEN, FEAT),...]
where the time goes in v3:
time: 97.4 us; the launch traced here: 97.3 us
  Pallas kernels  94.3 us (97%)
  local copies, waits for them, and re-layouts  3.05 us (3%)
    pallas_call x1, Pallas kernels, attend(): pl.pallas_call(kernel, out_shape=jax.ShapeDtypeStruct((REQS, QLEN, FEAT),...  94.3 us
    unnamed x1, local copies, waits for them, and re-layouts  3.05 us

profile of v3, /device:TPU:1, one launch (start us, length us, event | category | flops | bytes accessed | tf_op | source)
XLA Modules:
  0.0 97.3 jit_solution(9223694414201387133)
XLA Ops:
  0.0 94.3 %blend.1 = bf16[4,1024,256]{2,1,0:T(8,128)(2,1)} custom-call(bf16[4,1024,256]{2,1,0:T(8,128)(2,1)} %q_hbm.1, bf16[8,2,64,256]{3,2,1,0:T(8,128)(2,1)} %kv_hbm.1, bf16[512,512]{1,0:T(8,128)(2,1)} %bitcast.2, bf16[512,2,256]{2,1,0:T(2,128)(2,1)} %w_hbm.1, s32[16,64]{1,0:T(8,128)} %bitcast.3, s32[128]{0:T(128)} %home_hbm.1, s32[64]{0:T(128)} %counts_hbm.1, ...), custom_call_target="tpu_custom_call" | custom-call | flops 14000000000 | bytes 8000000 | tf_op jit(solution)/shard_map/blend/pallas_call | solution.py:528
  94.3 3.0 %copy.10 = bf16[4,1024,256]{2,1,0:T(8,128)(2,1)} copy(bf16[4,1024,256]{2,1,0:T(8,128)(2,1)} %blend.1) | data formatting | bytes 4194304

commit v4 on v3

--- a/solution.py
+++ b/solution.py
@@ -21,7 +21,7 @@
 FEAT = 256
 ROWS = REQS * SEL
 DEEP = 512
-QTILE = 256
+QTILE = 512
 MASKED = -1e28
 TO_BASE_TWO = HD ** (-0.5) * math.log2(math.e)
 
@@ -78,7 +78,6 @@
     q_hbm, kv_hbm, x_hbm, w_hbm, ids_hbm, home_hbm, counts_hbm, renewed_hbm, out_hbm,
     ids, home, counts, renewed, q, w_raw, packed, table, bias, x_own, x_all, w_all, k_near, v_near, k_send, v_send, k_all, v_all,
     mixed, top, total, projected, squares, part_send, part_recv, norm_send, norm_recv, fresh, result,
-    wide_q, wide_k, wide_v,
     local_sem, out_sem, kv1_send, kv1_recv, kv2_send, kv2_recv,
     own_send, own_recv, other_send, other_recv, side_send, side_recv, flow_send, flow_recv,
     lend_send, lend_recv, core_send, core_recv, sum_send, sum_recv,
@@ -290,8 +289,13 @@
                 piece = x_all.at[at * 2 + core, pl.ds(ROWS * part, ROWS)]
                 remote(piece, piece, core_send.at[at, part], core_recv.at[at, part], sibling).wait_send()
 
-    swap = remote(part_send, part_recv, sum_send.at[0], sum_recv.at[0], partner)
-    swap_norm = remote(norm_send, norm_recv, sum_send.at[1], sum_recv.at[1], partner)
+    def swap(half):
+        rows = pl.ds(256 * half, 256)
+        return remote(
+            part_send.at[rows], part_recv.at[rows], sum_send.at[half], sum_recv.at[half], partner
+        )
+
+    swap_norm = remote(norm_send, norm_recv, sum_send.at[2], sum_recv.at[2], partner)
 
     def k2(r, d):
         return remote(
@@ -392,12 +396,21 @@
                 top[r, pl.ds(first, QTILE), lanes] = jnp.broadcast_to(largest, (QTILE, HD))
                 total[r, pl.ds(first, QTILE), lanes] = jnp.broadcast_to(summed, (QTILE, HD))
 
-    def project(part):
-        projected[...] = jnp.zeros_like(projected)
+    def project(part, half):
+        rows = pl.ds(ROWS * part + 256 * half, 256)
+        summed = dot(x_all[0, rows, :], w_all[0], NN)
+        for b in range(1, 8):
+            summed = summed + dot(x_all[b, rows, :], w_all[b], NN)
+        return summed
+
+    def sum_squares(part):
+        squares[...] = jnp.zeros_like(squares)
 
         @pl.loop(0, 8)
         def _(b):
-            projected[...] += dot(x_all[b, pl.ds(ROWS * part, ROWS), :], w_all[b], NN)
+            wide = x_all[b, pl.ds(ROWS * part, ROWS), :].astype(jnp.float32)
+            wide = wide * wide
+            squares[...] += (wide[:, 0:128] + wide[:, 128:256]) + (wide[:, 256:384] + wide[:, 384:512])
 
     x_start()
     loads[0].wait()
@@ -427,6 +440,8 @@
     x_two(1)
     v1.finish()
     send_values(0, 1)
+    send_keys(1, 1)
+    send_values(1, 1)
     x_three(0)
     loads[3].wait()
     loads[6].wait()
@@ -436,46 +451,34 @@
     x_three(1)
     own.finish()
     side(3).start()
-    send_keys(1, 3)
-    send_values(1, 3)
+    send_keys(2, 2)
+    send_values(2, 2)
     x_relayed(1)
     attend_cached(0)
+    attend_cached(1)
+    x_relayed(0)
     x_ended(1)
     other.finish()
     for j in range(4):
         side(j, False).wait_recv()
     x_others(1)
 
-    norm_send[...] = jnp.zeros_like(norm_send)
-
-    @pl.loop(0, 8)
-    def _(b):
-        narrow = x_all[b, pl.ds(ROWS, ROWS), :]
-        norm_send[...] += dot(jnp.ones((8, DEEP), jnp.bfloat16), narrow * narrow, NT)
-
-    project(1)
-    part_send[...] = projected[...].astype(jnp.bfloat16)
-    swap.start()
+    for half in (0, 1):
+        part_send[pl.ds(256 * half, 256), :] = project(1, half).astype(jnp.bfloat16)
+        swap(half).start()
+    x_ended(0)
+    sum_squares(1)
+    turned = jnp.transpose(squares[...])
+    norm_send[...] = jnp.broadcast_to(jnp.sum(turned, axis=0, keepdims=True), norm_send.shape)
     swap_norm.start()
-    x_relayed(0)
-    attend_cached(1)
-    x_ended(0)
     x_others(0)
-    squares[...] = jnp.zeros_like(squares)
-
-    @pl.loop(0, 8)
-    def _(b):
-        wide = x_all[b, pl.ds(0, ROWS), :].astype(jnp.float32)
-        wide = wide * wide
-        squares[...] += (wide[:, 0:128] + wide[:, 128:256]) + (wide[:, 256:384] + wide[:, 384:512])
-
-    project(0)
-
-    @pl.loop(2, REQS)
-    def _(r):
-        attend_cached(r)
-
-    swap.wait_recv()
+    sum_squares(0)
+    for half in (0, 1):
+        projected[pl.ds(256 * half, 256), :] = project(0, half)
+    attend_cached(2)
+
+    for half in (0, 1):
+        swap(half).wait_recv()
     swap_norm.wait_recv()
     lent = jnp.transpose(jnp.broadcast_to(norm_recv[0:1, :], (HD, ROWS)))
     mean = (jnp.sum(squares[...], axis=-1, keepdims=True) + lent) * (1.0 / D)
@@ -488,7 +491,10 @@
         if i >= 2:
             fresh[:, pl.ds(at + HD, HD)] = jnp.ones((ROWS, HD), jnp.bfloat16)
 
-    @pl.loop(0, REQS)
+    def store_result(r):
+        return pltpu.make_async_copy(result.at[r], out_hbm.at[r], out_sem.at[r])
+
+    @pl.loop(0, 3)
     def _(r):
         rows = pl.ds(pl.multiple_of(r * SEL, SEL), SEL)
         for h in (0, 1):
@@ -501,7 +507,36 @@
             both = dot(exps.astype(jnp.bfloat16), fresh[rows, pl.ds(FEAT + h * 2 * HD, 2 * HD)], NN)
             attended = (mixed[r, :, lanes] * fade + both[:, 0:HD]) / (total[r, :, lanes] * fade + both[:, HD:])
             result[r, :, lanes] = attended.astype(jnp.bfloat16)
-        pltpu.make_async_copy(result.at[r], out_hbm.at[r], out_sem.at[r]).start()
+        store_result(r).start()
+
+    r = REQS - 1
+    for d in (1, 3, 2):
+        k2_arrived(r, d)
+        v2_arrived(r, d)
+
+    @pl.loop(0, QLEN // QTILE)
+    def _(t):
+        rows = pl.ds(pl.multiple_of(t * QTILE, QTILE), QTILE)
+        shift = bias[r]
+        for h in (0, 1):
+            lanes = pl.ds(h * HD, HD)
+            tail = pl.ds(r * SEL, SEL)
+            keys = k_all[r, :, :, :, lanes].reshape(SPAN, HD)
+            values = v_all[r, :, :, :, lanes].reshape(SPAN, HD)
+            scores = dot(q[r, rows, lanes], keys, NT) * TO_BASE_TWO + shift
+            extra = dot(q[r, rows, lanes], fresh[tail, lanes], NT) * TO_BASE_TWO
+            largest = jnp.maximum(
+                jnp.max(scores, axis=-1, keepdims=True), jnp.max(extra, axis=-1, keepdims=True)
+            )
+            exps = jnp.exp2(scores - largest)
+            more = jnp.exp2(extra - largest)
+            summed = jnp.sum(exps, axis=-1, keepdims=True) + jnp.sum(more, axis=-1, keepdims=True)
+            blend = dot(exps.astype(jnp.bfloat16), values, NN) + dot(
+                more.astype(jnp.bfloat16), fresh[tail, pl.ds(FEAT + h * 2 * HD, HD)], NN
+            )
+            result[r, rows, lanes] = (blend / summed).astype(jnp.bfloat16)
+
+    store_result(r).start()
 
     for ring in (k1, v1, own, other):
         ring.drain()
@@ -515,10 +550,11 @@
             v2(r, d).wait_send()
 
     x_drain()
-    swap.wait_send()
+    swap(0).wait_send()
+    swap(1).wait_send()
     swap_norm.wait_send()
     for r in range(REQS):
-        pltpu.make_async_copy(result.at[r], out_hbm.at[r], out_sem.at[r]).wait()
+        store_result(r).wait()
 
 
 def attend(q, kv, rows, weights, ids, home, counts, renewed):
@@ -560,9 +596,6 @@
             pltpu.VMEM((8, ROWS), f32),
             pltpu.VMEM((ROWS, 3 * FEAT), bf),
             pltpu.VMEM((REQS, QLEN, FEAT), bf),
-            pltpu.VMEM((2, QLEN, 2 * HD), bf),
-            pltpu.VMEM((2, SPAN, 2 * HD), bf),
-            pltpu.VMEM((2, SPAN, 2 * HD), bf),
             dma((11,)),
             dma((REQS,)),
             dma((2, 4)), dma((2, 4)),
@@ -573,7 +606,7 @@
             dma((2, 2, 4)), dma((2, 2, 4)),
             dma((2,)), dma((2,)),
             dma((4, 2)), dma((4, 2)),
-            dma((2,)), dma((2,)),
+            dma((3,)), dma((3,)),
         ],
         compiler_params=pltpu.CompilerParams(
             collective_id=0, has_side_effects=True, vmem_limit_bytes=60 * 1024 * 1024

time: 97.4 us -> 93.6 us (0.961)
  Pallas kernels: 94.3 us -> 90.5 us
    pallas_call x1, Pallas kernels: 94.3 us -> 90.5 us  [attend(): pl.pallas_call(kernel, out_shape=jax.ShapeDtypeStruct((REQS, QLEN, FEAT),...]
where the time goes in v4:
time: 93.6 us; the launch traced here: 93.5 us
  Pallas kernels  90.5 us (97%)
  local copies, waits for them, and re-layouts  3.05 us (3%)
    pallas_call x1, Pallas kernels, attend(): pl.pallas_call(kernel, out_shape=jax.ShapeDtypeStruct((REQS, QLEN, FEAT),...  90.5 us
    unnamed x1, local copies, waits for them, and re-layouts  3.05 us

profile of v4, /device:TPU:1, one launch (start us, length us, event | category | flops | bytes accessed | tf_op | source)
XLA Modules:
  0.0 93.5 jit_solution(1444890154154460903)
XLA Ops:
  0.0 90.5 %blend.1 = bf16[4,1024,256]{2,1,0:T(8,128)(2,1)} custom-call(bf16[4,1024,256]{2,1,0:T(8,128)(2,1)} %q_hbm.1, bf16[8,2,64,256]{3,2,1,0:T(8,128)(2,1)} %kv_hbm.1, bf16[512,512]{1,0:T(8,128)(2,1)} %bitcast.2, bf16[512,2,256]{2,1,0:T(2,128)(2,1)} %w_hbm.1, s32[16,64]{1,0:T(8,128)} %bitcast.3, s32[128]{0:T(128)} %home_hbm.1, s32[64]{0:T(128)} %counts_hbm.1, ...), custom_call_target="tpu_custom_call" | custom-call | flops 14000000000 | bytes 8000000 | tf_op jit(solution)/shard_map/blend/pallas_call | solution.py:564
  90.5 3.0 %copy.10 = bf16[4,1024,256]{2,1,0:T(8,128)(2,1)} copy(bf16[4,1024,256]{2,1,0:T(8,128)(2,1)} %blend.1) | data formatting | bytes 4194304

commit v5 on v4

--- a/solution.py
+++ b/solution.py
@@ -169,10 +169,11 @@
             lend_send.at[half], lend_recv.at[half], partner,
         )
 
-    def to_core(dist, part, mine=True):
+    def to_core(dist, *pieces):
         at = (z + 8 + dist) % 8
-        piece = x_all.at[(at // 2) * 2 + (core if mine else 1 - core), pl.ds(ROWS * part, ROWS)]
-        return remote(piece, piece, core_send.at[at // 2, part], core_recv.at[at // 2, part], sibling)
+        for w in pieces:
+            piece = x_all.at[(at // 2) * 2 + core, pl.ds(256 * w, 256)]
+            remote(piece, piece, core_send.at[at // 2, w], core_recv.at[at // 2, w], sibling).start()
 
     def x_start():
         @pl.when(source)
@@ -181,7 +182,7 @@
             for w in (0, 1):
                 flow(0, 0, 0, w).start()
                 flow(1, 0, 0, w).start()
-            to_core(0, 0).start()
+            to_core(0, 0, 1)
 
         @pl.when(relay)
         def _():
@@ -196,8 +197,8 @@
                 for way in (0, 1):
                     flow(way, 0, 1, w).wait_recv()
                     flow(way, 0, 1, w).start()
-            to_core(-1, 0).start()
-            to_core(1, 0).start()
+            to_core(-1, 0, 1)
+            to_core(1, 0, 1)
 
         @pl.when(source)
         def _():
@@ -205,7 +206,7 @@
                 lend(w - 2).wait_recv()
                 flow(0, 0, 0, w).start()
                 flow(1, 0, 0, w).start()
-            to_core(0, 1).start()
+            to_core(0, 2, 3)
 
     def x_two(half):
         w = 2 + half
@@ -216,16 +217,16 @@
                 flow(way, 0, 1, w).wait_recv()
                 flow(way, 0, 1, w).start()
             if half:
-                to_core(-1, 1).start()
-                to_core(1, 1).start()
+                to_core(-1, 2, 3)
+                to_core(1, 2, 3)
 
         @pl.when(source)
         def _():
             for way in (0, 1):
                 flow(way, 0, 2, half).wait_recv()
             if half:
-                to_core(-2, 0).start()
-                to_core(2, 0).start()
+                to_core(-2, 0, 1)
+                to_core(2, 0, 1)
 
     def x_three(half):
         w = 2 + half
@@ -239,8 +240,8 @@
                 for way in (0, 1):
                     flow(way, 1, 2, 0).start()
                     flow(way, 1, 2, 1).start()
-                to_core(-2, 1).start()
-                to_core(2, 1).start()
+                to_core(-2, 2, 3)
+                to_core(2, 2, 3)
 
     def x_relayed(part):
         @pl.when(relay)
@@ -251,20 +252,19 @@
                     flow(way, 1, 3, w).wait_recv()
                     if way == half:
                         flow(way, 1, 3, w).start()
-            to_core(-3, part).start()
-            to_core(3, part).start()
-
-    def x_ended(part):
+                to_core(-3, w)
+                to_core(3, w)
+
+    def x_ended(w):
         @pl.when(source)
         def _():
-            for way in (0, 1):
-                flow(way, 1, 4, 2 * part + way).wait_recv()
-            to_core(4, part).start()
-
-    def x_others(part):
+            flow(w % 2, 1, 4, w).wait_recv()
+            to_core(4, w)
+
+    def x_others(w):
         for at in range(4):
-            piece = x_all.at[at * 2 + 1 - core, pl.ds(ROWS * part, ROWS)]
-            remote(piece, piece, core_send.at[at, part], core_recv.at[at, part], sibling).wait_recv()
+            piece = x_all.at[at * 2 + 1 - core, pl.ds(256 * w, 256)]
+            remote(piece, piece, core_send.at[at, w], core_recv.at[at, w], sibling).wait_recv()
 
     def x_drain():
         @pl.when(source)
@@ -285,9 +285,9 @@
                     flow(way, 1, 3, 2 * part + way).wait_send()
 
         for at in range(4):
-            for part in (0, 1):
-                piece = x_all.at[at * 2 + core, pl.ds(ROWS * part, ROWS)]
-                remote(piece, piece, core_send.at[at, part], core_recv.at[at, part], sibling).wait_send()
+            for w in range(4):
+                piece = x_all.at[at * 2 + core, pl.ds(256 * w, 256)]
+                remote(piece, piece, core_send.at[at, w], core_recv.at[at, w], sibling).wait_send()
 
     def swap(half):
         rows = pl.ds(256 * half, 256)
@@ -440,8 +440,6 @@
     x_two(1)
     v1.finish()
     send_values(0, 1)
-    send_keys(1, 1)
-    send_values(1, 1)
     x_three(0)
     loads[3].wait()
     loads[6].wait()
@@ -451,27 +449,31 @@
     x_three(1)
     own.finish()
     side(3).start()
-    send_keys(2, 2)
-    send_values(2, 2)
+    send_keys(1, 3)
+    send_values(1, 3)
     x_relayed(1)
     attend_cached(0)
-    attend_cached(1)
-    x_relayed(0)
-    x_ended(1)
+    x_ended(2)
     other.finish()
     for j in range(4):
         side(j, False).wait_recv()
-    x_others(1)
-
-    for half in (0, 1):
-        part_send[pl.ds(256 * half, 256), :] = project(1, half).astype(jnp.bfloat16)
-        swap(half).start()
-    x_ended(0)
+    x_others(2)
+    part_send[pl.ds(0, 256), :] = project(1, 0).astype(jnp.bfloat16)
+    swap(0).start()
+    x_ended(3)
+    x_others(3)
+    part_send[pl.ds(256, 256), :] = project(1, 1).astype(jnp.bfloat16)
+    swap(1).start()
+    x_relayed(0)
     sum_squares(1)
     turned = jnp.transpose(squares[...])
     norm_send[...] = jnp.broadcast_to(jnp.sum(turned, axis=0, keepdims=True), norm_send.shape)
     swap_norm.start()
+    attend_cached(1)
+    x_ended(0)
+    x_ended(1)
     x_others(0)
+    x_others(1)
     sum_squares(0)
     for half in (0, 1):
         projected[pl.ds(256 * half, 256), :] = project(0, half)
@@ -605,7 +607,7 @@
             dma((5,)), dma((5,)),
             dma((2, 2, 4)), dma((2, 2, 4)),
             dma((2,)), dma((2,)),
-            dma((4, 2)), dma((4, 2)),
+            dma((4, 4)), dma((4, 4)),
             dma((3,)), dma((3,)),
         ],
         compiler_params=pltpu.CompilerParams(

time: 93.6 us -> 92 us (0.983)
  Pallas kernels: 90.5 us -> 88.8 us
    pallas_call x1, Pallas kernels: 90.5 us -> 88.8 us  [attend(): pl.pallas_call(kernel, out_shape=jax.ShapeDtypeStruct((REQS, QLEN, FEAT),...]
where the time goes in v5:
time: 92 us; the launch traced here: 91.9 us
  Pallas kernels  88.8 us (97%)
  local copies, waits for them, and re-layouts  3.05 us (3%)
    pallas_call x1, Pallas kernels, attend(): pl.pallas_call(kernel, out_shape=jax.ShapeDtypeStruct((REQS, QLEN, FEAT),...  88.8 us
    unnamed x1, local copies, waits for them, and re-layouts  3.05 us

profile of v5, /device:TPU:1, one launch (start us, length us, event | category | flops | bytes accessed | tf_op | source)
XLA Modules:
  0.0 91.9 jit_solution(7634201494351360857)
XLA Ops:
  0.0 88.8 %blend.1 = bf16[4,1024,256]{2,1,0:T(8,128)(2,1)} custom-call(bf16[4,1024,256]{2,1,0:T(8,128)(2,1)} %q_hbm.1, bf16[8,2,64,256]{3,2,1,0:T(8,128)(2,1)} %kv_hbm.1, bf16[512,512]{1,0:T(8,128)(2,1)} %bitcast.2, bf16[512,2,256]{2,1,0:T(2,128)(2,1)} %w_hbm.1, s32[16,64]{1,0:T(8,128)} %bitcast.3, s32[128]{0:T(128)} %home_hbm.1, s32[64]{0:T(128)} %counts_hbm.1, ...), custom_call_target="tpu_custom_call" | custom-call | flops 14000000000 | bytes 8000000 | tf_op jit(solution)/shard_map/blend/pallas_call | solution.py:566
  88.9 3.0 %copy.10 = bf16[4,1024,256]{2,1,0:T(8,128)(2,1)} copy(bf16[4,1024,256]{2,1,0:T(8,128)(2,1)} %blend.1) | data formatting | bytes 4194304

commit v6 on v5

--- a/solution.py
+++ b/solution.py
@@ -477,7 +477,6 @@
     sum_squares(0)
     for half in (0, 1):
         projected[pl.ds(256 * half, 256), :] = project(0, half)
-    attend_cached(2)
 
     for half in (0, 1):
         swap(half).wait_recv()
@@ -496,7 +495,7 @@
     def store_result(r):
         return pltpu.make_async_copy(result.at[r], out_hbm.at[r], out_sem.at[r])
 
-    @pl.loop(0, 3)
+    @pl.loop(0, 2)
     def _(r):
         rows = pl.ds(pl.multiple_of(r * SEL, SEL), SEL)
         for h in (0, 1):
@@ -511,34 +510,35 @@
             result[r, :, lanes] = attended.astype(jnp.bfloat16)
         store_result(r).start()
 
-    r = REQS - 1
-    for d in (1, 3, 2):
-        k2_arrived(r, d)
-        v2_arrived(r, d)
-
-    @pl.loop(0, QLEN // QTILE)
-    def _(t):
-        rows = pl.ds(pl.multiple_of(t * QTILE, QTILE), QTILE)
-        shift = bias[r]
-        for h in (0, 1):
-            lanes = pl.ds(h * HD, HD)
-            tail = pl.ds(r * SEL, SEL)
-            keys = k_all[r, :, :, :, lanes].reshape(SPAN, HD)
-            values = v_all[r, :, :, :, lanes].reshape(SPAN, HD)
-            scores = dot(q[r, rows, lanes], keys, NT) * TO_BASE_TWO + shift
-            extra = dot(q[r, rows, lanes], fresh[tail, lanes], NT) * TO_BASE_TWO
-            largest = jnp.maximum(
-                jnp.max(scores, axis=-1, keepdims=True), jnp.max(extra, axis=-1, keepdims=True)
-            )
-            exps = jnp.exp2(scores - largest)
-            more = jnp.exp2(extra - largest)
-            summed = jnp.sum(exps, axis=-1, keepdims=True) + jnp.sum(more, axis=-1, keepdims=True)
-            blend = dot(exps.astype(jnp.bfloat16), values, NN) + dot(
-                more.astype(jnp.bfloat16), fresh[tail, pl.ds(FEAT + h * 2 * HD, HD)], NN
-            )
-            result[r, rows, lanes] = (blend / summed).astype(jnp.bfloat16)
-
-    store_result(r).start()
+    @pl.loop(2, REQS)
+    def _(r):
+        for d in (1, 3, 2):
+            k2_arrived(r, d)
+            v2_arrived(r, d)
+
+        @pl.loop(0, QLEN // QTILE)
+        def _(t):
+            rows = pl.ds(pl.multiple_of(t * QTILE, QTILE), QTILE)
+            shift = bias[r]
+            for h in (0, 1):
+                lanes = pl.ds(h * HD, HD)
+                tail = pl.ds(pl.multiple_of(r * SEL, SEL), SEL)
+                keys = k_all[r, :, :, :, lanes].reshape(SPAN, HD)
+                values = v_all[r, :, :, :, lanes].reshape(SPAN, HD)
+                scores = dot(q[r, rows, lanes], keys, NT) * TO_BASE_TWO + shift
+                extra = dot(q[r, rows, lanes], fresh[tail, lanes], NT) * TO_BASE_TWO
+                largest = jnp.maximum(
+                    jnp.max(scores, axis=-1, keepdims=True), jnp.max(extra, axis=-1, keepdims=True)
+                )
+                exps = jnp.exp2(scores - largest)
+                more = jnp.exp2(extra - largest)
+                summed = jnp.sum(exps, axis=-1, keepdims=True) + jnp.sum(more, axis=-1, keepdims=True)
+                blend = dot(exps.astype(jnp.bfloat16), values, NN) + dot(
+                    more.astype(jnp.bfloat16), fresh[tail, pl.ds(FEAT + h * 2 * HD, HD)], NN
+                )
+                result[r, rows, lanes] = (blend / summed).astype(jnp.bfloat16)
+
+        store_result(r).start()
 
     for ring in (k1, v1, own, other):
         ring.drain()

time: 92 us -> 91.4 us (level)
  no operation moved by 1% of the time
where the time goes in v6:
time: 91.4 us; the launch traced here: 91.1 us
  Pallas kernels  88.1 us (96%)
  local copies, waits for them, and re-layouts  3.05 us (3%)
    pallas_call x1, Pallas kernels, attend(): pl.pallas_call(kernel, out_shape=jax.ShapeDtypeStruct((REQS, QLEN, FEAT),...  88.1 us
    unnamed x1, local copies, waits for them, and re-layouts  3.05 us

profile of v6, /device:TPU:1, one launch (start us, length us, event | category | flops | bytes accessed | tf_op | source)
XLA Modules:
  0.0 91.1 jit_solution(11446913415193661851)
XLA Ops:
  0.0 88.1 %blend.1 = bf16[4,1024,256]{2,1,0:T(8,128)(2,1)} custom-call(bf16[4,1024,256]{2,1,0:T(8,128)(2,1)} %q_hbm.1, bf16[8,2,64,256]{3,2,1,0:T(8,128)(2,1)} %kv_hbm.1, bf16[512,512]{1,0:T(8,128)(2,1)} %bitcast.2, bf16[512,2,256]{2,1,0:T(2,128)(2,1)} %w_hbm.1, s32[16,64]{1,0:T(8,128)} %bitcast.3, s32[128]{0:T(128)} %home_hbm.1, s32[64]{0:T(128)} %counts_hbm.1, ...), custom_call_target="tpu_custom_call" | custom-call | flops 14000000000 | bytes 8000000 | tf_op jit(solution)/shard_map/blend/pallas_call | solution.py:566
  88.1 3.0 %copy.10 = bf16[4,1024,256]{2,1,0:T(8,128)(2,1)} copy(bf16[4,1024,256]{2,1,0:T(8,128)(2,1)} %blend.1) | data formatting | bytes 4194304
